TPU v7x, 128 devices: a whole 4x4x4 slice. The times are simulated.
128 devices in a mesh: src: 4 (over y), tile: 32 (over z, x, core).
Axes of the slice: x: 4, y: 4, z: 4, core: 2. Of those that a mesh axis runs over, the one named last changes fastest.
Arguments:
- exposure: bfloat16 [4, 4096, 8192], P('src', 'tile'), may hold values from -6 to 6
- row_bases: bfloat16 [27, 41], replicated, may hold values from -1 to 1
- col_bases: bfloat16 [27, 41], replicated, may hold values from -1 to 1
- coefficients: float32 [4, 32, 64, 27], P('src', 'tile'), may hold values from -1.2 to 1.2
- warp_rows: bfloat16 [4, 32, 64, 128, 128], P('src', 'tile'), may hold values from -0.4 to 1.4, as said below
- warp_cols: bfloat16 [4, 32, 64, 128, 128], P('src', 'tile'), may hold values from -0.4 to 1.4, as said below
- variance: float32 [4, 32, 64], P('src', 'tile'), may hold values from 0.25 to 4
- footprint: int32 [4, 32, 64, 1], P('src', 'tile'), may hold values from 0 to 31; in each aligned block of 64 rows (0 to 63, 64 to 127, ..., all dimensions but the last counted through in order) at most 4 rows name the same one
- slot_index: int32 [4, 32, 64], P('src', 'tile'), may hold values from 0 to 63
Outputs:
- coadd: float32 [128, 512, 512], P('tile', 'src')
Inputs may be any that keep to these rules, and one draw needn't show every extreme that they name: `footprint`: within the blocks of one index of src and tile, no tile owner is named more than 4 times, a bound that some block reaches. `warp_rows`: each row holds the Lanczos weights of one output pixel. `warp_cols`: each row holds the Lanczos weights of one output pixel.
All inputs are finite; a program needn't handle non-finite values.
Results may differ from a plain program's by a relative error of at most 0.014.
Values may be sent and summed in bfloat16 or wider, within the bound.
A program may use at most 128 MiB of HBM per device.

v0:
```python
import jax
import jax.numpy as jnp
from jax import lax
from jax.sharding import PartitionSpec as P

TILES_DEV = 4


def with_halo(array, sides, width):
    for axis, dim in sides:
        count, length = (lax.axis_size(axis), array.shape[dim])
        up = [(i, (i + 1) % count) for i in range(count - 1)]
        down = [(j, i) for i, j in up]
        last = lax.slice_in_dim(array, length - width, length, axis=dim)
        initial = lax.slice_in_dim(array, 0, width, axis=dim)
        before = lax.ppermute(last, axis, up)
        after = lax.ppermute(initial, axis, down)
        array = jnp.concatenate([before, array, after], axis=dim)
    return array


def banded(tap_table, rows_out, rows_in):
    tap_total = tap_table.shape[-1]
    grid_shape = (tap_total, rows_out, rows_in)
    offset = lax.broadcasted_iota(jnp.int32, grid_shape, 2) - lax.broadcasted_iota(
        jnp.int32, grid_shape, 1
    )
    tap_index = lax.broadcasted_iota(jnp.int32, grid_shape, 0)
    selector = (offset == tap_index).astype(jnp.bfloat16)
    return jnp.einsum(
        "kt,toi->koi", tap_table, selector, preferred_element_type=jnp.float32
    ).astype(jnp.bfloat16)


def match_strip(padded, vertical, block_coefficients, col_bases):
    basis_count, tap_count = col_bases.shape
    block_side = vertical.shape[1]
    span = vertical.shape[2]
    group_total = block_coefficients.shape[0] // 4

    def one_group(group_id):
        portion = lax.dynamic_slice_in_dim(
            padded, group_id * 4 * block_side, 3 * block_side + span, 1
        )
        vertical_pass = jnp.einsum(
            "kor,rc->koc", vertical, portion, preferred_element_type=jnp.float32
        ).astype(jnp.bfloat16)
        windows = jnp.stack(
            [
                vertical_pass[:, :, column * block_side : column * block_side + span]
                for column in range(4)
            ],
            2,
        )
        weights = lax.dynamic_slice_in_dim(block_coefficients, group_id * 4, 4, 0)
        kernels = (weights[:, :, None] * col_bases.astype(jnp.float32)[None]).astype(jnp.bfloat16)
        across = banded(kernels.reshape(4 * basis_count, tap_count), block_side, span).reshape(
            4, basis_count, block_side, span
        )
        return jnp.einsum(
            "kobw,bkcw->boc", windows, across, preferred_element_type=jnp.float32
        ).astype(jnp.bfloat16)

    return lax.map(one_group, jnp.arange(group_total, dtype=jnp.int32)).reshape(
        -1, block_side, block_side
    )


def route_blocks(warped, weight, target_peer, slot_value, peer_count, capacity):
    block_count = warped.shape[0]
    pair_shape = (block_count, block_count)
    earlier = lax.broadcasted_iota(jnp.int32, pair_shape, 1) < lax.broadcasted_iota(
        jnp.int32, pair_shape, 0
    )
    same_peer = (target_peer[:, None] == target_peer[None, :]) & earlier
    rank_among = jnp.sum(same_peer.astype(jnp.int32), axis=1)
    position = target_peer * capacity + rank_among
    buffer_shape = (peer_count * capacity, block_count)
    buffer_slot = lax.broadcasted_iota(jnp.int32, buffer_shape, 0)
    matches = buffer_slot == position[None, :]
    found = jnp.sum(matches.astype(jnp.int32), axis=1)
    source_row = jnp.sum(
        jnp.where(matches, lax.broadcasted_iota(jnp.int32, buffer_shape, 1), 0), axis=1
    ) + block_count * (1 - found)
    padded_blocks = jnp.concatenate([warped, jnp.zeros((1,) + warped.shape[1:], warped.dtype)], 0)
    metadata = jnp.stack([weight.astype(jnp.float32), slot_value.astype(jnp.float32)], 1)
    metadata = jnp.concatenate([metadata, jnp.zeros((1, 2), jnp.float32)], 0).astype(jnp.bfloat16)
    return (padded_blocks[source_row], metadata[source_row])


def accumulate(incoming, arrived, slot_total):
    received = incoming.shape[0]
    weight = arrived[:, 0]
    slot_value = arrived[:, 1].astype(jnp.float32)
    slot_number = lax.broadcasted_iota(jnp.int32, (slot_total, received), 0).astype(jnp.float32)
    slot_table = jnp.where(
        slot_number == slot_value[None, :], weight[None, :], jnp.zeros((), jnp.bfloat16)
    )
    numerator = jnp.dot(
        slot_table, incoming.reshape(received, -1), preferred_element_type=jnp.float32
    )
    denominator = jnp.sum(slot_table.astype(jnp.float32), axis=1)
    return (numerator, denominator)


def normalize_tiles(numerator, denominator, tiles_dev, blocks_across, block_side):
    shaped = numerator.reshape(tiles_dev, blocks_across, block_side, block_side)
    scaled = shaped / jnp.maximum(denominator, 1.0).reshape(tiles_dev, blocks_across, 1, 1)
    return scaled.transpose(0, 2, 1, 3).reshape(tiles_dev, block_side, blocks_across * block_side)


def body(
    exposure,
    row_bases,
    col_bases,
    coefficients,
    warp_rows,
    warp_cols,
    variance,
    footprint,
    slot_index,
):
    block_side = warp_rows.shape[-1]
    half_reach = row_bases.shape[1] // 2
    src_count = lax.axis_size("src")
    tile_count = lax.axis_size("tile")
    block_count = warp_rows.shape[2]
    capacity = max(2, 2 * block_count // tile_count)
    strip_rows = with_halo(exposure[0], (("tile", 0),), half_reach)
    padded = jnp.pad(strip_rows, ((0, 0), (half_reach, half_reach)))
    vertical = banded(row_bases, block_side, block_side + 2 * half_reach)
    matched = match_strip(padded, vertical, coefficients[0, 0], col_bases)
    across = jnp.einsum(
        "bor,brc->boc", warp_rows[0, 0], matched, preferred_element_type=jnp.float32
    ).astype(jnp.bfloat16)
    warped = jnp.einsum(
        "boc,bpc->bop", across, warp_cols[0, 0], preferred_element_type=jnp.float32
    ).astype(jnp.bfloat16)
    weight = (1.0 / variance[0, 0]).astype(jnp.bfloat16)
    target_tile = footprint[0, 0, :, 0]
    slot_value = slot_index[0, 0]
    per_tile = src_count * src_count
    outgoing, metadata = route_blocks(warped, weight, target_tile, slot_value, tile_count, capacity)
    incoming, arrived = (
        lax.all_to_all(outgoing, "tile", split_axis=0, concat_axis=0, tiled=True),
        lax.all_to_all(metadata, "tile", split_axis=0, concat_axis=0, tiled=True),
    )
    partial_num, partial_den = accumulate(incoming, arrived, TILES_DEV * per_tile)
    numerator, denominator = (
        lax.psum_scatter(
            partial_num.reshape(TILES_DEV, src_count, src_count, -1).astype(jnp.bfloat16),
            "src",
            scatter_dimension=1,
            tiled=True,
        ).astype(jnp.float32),
        lax.psum_scatter(
            partial_den.reshape(TILES_DEV, src_count, src_count).astype(jnp.bfloat16),
            "src",
            scatter_dimension=1,
            tiled=True,
        ).astype(jnp.float32),
    )
    return normalize_tiles(numerator, denominator, TILES_DEV, src_count, block_side)


def solution(mesh):
    placed = (
        P("src", "tile", None),
        P(),
        P(),
        P("src", "tile", None, None),
        P("src", "tile", None, None, None),
        P("src", "tile", None, None, None),
        P("src", "tile", None),
        P("src", "tile", None, None),
        P("src", "tile", None),
    )
    return jax.shard_map(
        body, mesh=mesh, in_specs=placed, out_specs=P("tile", "src", None), check_vma=False
    )
```

profile of v0, /device:TPU:3, one launch (start us, length us, event | category | flops | bytes accessed | tf_op | source)
XLA Modules:
  0.0 401.1 jit_solution(3604480917651916869)
XLA Ops:
  8.8 2.7 collective-permute-start.1
  11.5 3.0 collective-permute-start
  19.3 9.9 %all-to-all-start = ((bf16[32,4,2]{1,2,0:T(2,128)(2,1)}), bf16[32,4,2]{1,2,0:T(2,128)(2,1)}, u32[]{:S(2)}, u32[]{:S(2)}) async-start(bf16[32,4,2]{1,2,0:T(2,128)(2,1)} %copy.39), calls=%async_computation | async-start | bytes 32768 | tf_op jit(solution)/shard_map/all_to_all | solution.py:146
  31.5 5.1 %fusion.36 = bf16[168,8232]{1,0:T(8,128)(2,1)} fusion(bf16[20,8192]{1,0:T(8,128)(2,1)} %collective-permute-done.1, bf16[128,8192]{1,0:T(8,128)(2,1)} %bitcast.120, bf16[20,8192]{1,0:T(8,128)(2,1)} %collective-permute-done), kind=kLoop, calls=%fused_computation.41 | loop fusion | flops 16595712 | bytes 5518464 | tf_op jit(solution)/shard_map/concatenate | solution.py:18
  36.6 209.4 %while.12 = (s32[]{:T(128)}, bf16[16,4,128,128]{3,2,1,0:T(8,128)(2,1)}, s32[16]{0:T(128)S(1)}, bf16[168,8232]{1,0:T(8,128)(2,1)}, bf16[27,128,168]{1,2,0:T(8,128...) while((s32[]{:T(128)}, ...), condition=%wide.region_4.5_spmd, body=%wide.region_3.4_spmd.sunk | while | flops 1439008384 | bytes 51846908 | solution.py:64
  39.5 3.3 copy.57
  52.6 3.3 copy.57
  65.7 3.3 copy.57
  78.8 3.3 copy.57
  91.8 3.3 copy.57
  104.9 3.3 copy.57
  112.4 2.7 fusion.80
  118.0 3.3 copy.57
  125.5 2.7 fusion.80
  131.1 3.3 copy.57
  144.2 3.3 copy.57
  157.3 3.3 copy.57
  170.4 3.3 copy.57
  183.5 3.3 copy.57
  196.6 3.3 copy.57
  209.6 3.3 copy.57
  222.7 3.3 copy.57
  235.8 3.3 copy.57
  246.0 6.5 %fusion.46 = bf16[64,128,128]{2,1,0:T(8,128)(2,1)} fusion(bf16[1,1,64,128,128]{4,3,2,1,0:T(8,128)(2,1)S(1)} %copy-done, bf16[64,128,128]{2,1,0:T(8,128)(2,1)} %bitcast.121, bf16[1,1,64,128,128]{4,3,2,1,0:T(8,128)(2,1)} %param.15), kind=kOutput, calls=%fused_computation.47 | convolution fusion | flops 538968064 | bytes 8388608 | tf_op jit(solution)/shard_map/boc,bpc->bop/dot_general | solution.py:136
  252.5 3.2 concatenate.11
  255.7 4.7 %gather_fusion.1 = bf16[128,128,128]{2,1,0:T(8,128)(2,1)} fusion(bf16[65,128,128]{2,1,0:T(8,128)(2,1)} %concatenate.11, s32[1024]{0:T(1024)} %copy-done.3), kind=kCustom, calls=%fused_computation.1 | custom fusion | bytes 8389120 | tf_op jit(solution)/shard_map/gather | solution.py:88
  260.4 7.4 %all-to-all-start.1 = ((bf16[128,128,128]{2,1,0:T(8,128)(2,1)}), bf16[128,128,128]{2,1,0:T(8,128)(2,1)}, u32[]{:S(2)}, u32[]{:S(2)}) async-start(bf16[128,128,128]{2,1,0:T(8,128)(2,1)} %gather_fusion.1), calls=%async_computation.1 | async-start | bytes 8388608 | tf_op jit(solution)/shard_map/all_to_all | solution.py:145
  268.8 49.9 %all-to-all-done.1 = bf16[128,128,128]{2,1,0:T(8,128)(2,1)} async-done(((bf16[128,128,128]{2,1,0:T(8,128)(2,1)}), bf16[128,128,128]{2,1,0:T(8,128)(2,1)}, u32[]{:S(2)}, u32[]{:S(2)}) %all-to-all-start.1) | async-done | bytes 4194336 | tf_op jit(solution)/shard_map/all_to_all | solution.py:145
  318.7 7.3 %reshape.179 = bf16[128,16384,1,1]{1,0,2,3:T(8,128)(2,1)} reshape(bf16[128,128,128]{2,1,0:T(8,128)(2,1)} %all-to-all-done.1) | data formatting | bytes 8388608 | tf_op jit(solution)/shard_map/reshape | solution.py:100
  325.9 4.6 %convolution_convert_fusion = bf16[4,4,4,16384]{3,2,1,0:T(4,128)(2,1)} fusion(bf16[128,16384,1,1]{1,0,2,3:T(8,128)(2,1)} %reshape.179, f32[128]{0:T(128)S(1)} %get-tuple-element.146, f32[4,4,4]{2,1,0:T(4,128)S(1)} %add_convert_fusion, bf16[128]{0:T(256)(128)(2,1)S(1)} %get-tuple-element.145), kind=kOutput, calls=%fused_computation.30 | convolution fusion | flops 269500416 | bytes 6292480 | tf_op jit(solution)/shard_map/dot_general | solution.py:99
  331.4 8.7 %all-reduce.4 = bf16[4,4,4]{2,0,1:T(4,128)(2,1)S(1)} all-reduce(bf16[4,4,4]{2,0,1:T(4,128)(2,1)S(1)} %copy.46), channel_id=3, replica_groups=mesh['src'=4,'tile'=32] {'src'}, use_global_device_ids=true, to_apply=%region_7.8.clone | all-reduce | flops 64 | bytes 256
  340.7 47.8 %all-reduce.7.cloned.1.call-done = bf16[4,4,4,16384]{3,2,1,0:T(4,128)(2,1)} async-done(((bf16[4,4,4,16384]{3,2,1,0:T(4,128)(2,1)}), bf16[4,4,4,16384]{3,2,1,0:T(4,128)(2,1)}) %all-reduce.7.cloned.1.call-update) | async-done | bytes 2097168
  (269 shorter events, 146.7 us)
Async XLA Ops:
  6.5 239.4 %copy-start = (bf16[1,1,64,128,128]{4,3,2,1,0:T(8,128)(2,1)S(1)}, bf16[1,1,64,128,128]{4,3,2,1,0:T(8,128)(2,1)}, u32[]{:S(2)}) copy-start(bf16[1,1,64,128,128]{4,3,2,1,0:T(8,128)(2,1)} %param.16) | copy-start | bytes 6291460
  8.7 22.5 %copy-start.1 = (f32[1,1,64,27]{2,1,3,0:T(1,128)S(1)}, f32[1,1,64,27]{2,1,3,0:T(1,128)}, u32[]{:S(2)}) copy-start(f32[1,1,64,27]{2,1,3,0:T(1,128)} %param.14) | copy-start | bytes 20740
  8.8 22.6 %copy-start.2 = (bf16[27,41]{1,0:T(8,128)(2,1)S(1)}, bf16[27,41]{1,0:T(8,128)(2,1)}, u32[]{:S(2)}) copy-start(bf16[27,41]{1,0:T(8,128)(2,1)} %param.13) | copy-start | bytes 6646
  8.8 22.7 %collective-permute-start.1 = (bf16[20,8192]{1,0:T(8,128)(2,1)}, bf16[20,8192]{1,0:T(8,128)(2,1)}, u32[]{:S(2)}, u32[]{:S(2)}) collective-permute-start(bf16[20,8192]{1,0:T(8,128)(2,1)} %get-tuple-element.144), channel_id=1, source_target_pairs={{1,0},{2,1},{3,2},{4,3},{5,4},{6,5},{7,6},{8,7},{9,8},{10,9},{11,1... | collective-permute-start | bytes 983048 | tf_op jit(solution)/shard_map/ppermute | solution.py:17
  11.5 20.0 %collective-permute-start = (bf16[20,8192]{1,0:T(8,128)(2,1)}, bf16[20,8192]{1,0:T(8,128)(2,1)}, u32[]{:S(2)}, u32[]{:S(2)}) collective-permute-start(bf16[20,8192]{1,0:T(8,128)(2,1)} %get-tuple-element.143), channel_id=1, source_target_pairs={{0,1},{1,2},{2,3},{3,4},{4,5},{5,6},{6,7},{7,8},{8,9},{9,10},{10,1... | collective-permute-start | bytes 983048 | tf_op jit(solution)/shard_map/ppermute | solution.py:16
  17.7 11.6 %copy-start.3 = (s32[1024]{0:T(1024)}, s32[1024]{0:T(1024)S(1)}, u32[]{:S(2)}) copy-start(s32[1024]{0:T(1024)S(1)} %pad_clamp_fusion) | copy-start | bytes 12292
  19.3 241.1 %all-to-all-start = ((bf16[32,4,2]{1,2,0:T(2,128)(2,1)}), bf16[32,4,2]{1,2,0:T(2,128)(2,1)}, u32[]{:S(2)}, u32[]{:S(2)}) async-start(bf16[32,4,2]{1,2,0:T(2,128)(2,1)} %copy.39), calls=%async_computation | async-start | bytes 32768 | tf_op jit(solution)/shard_map/all_to_all | solution.py:146
  43.5 2.9 slice-start
  46.0 1.0 slice-start.1
  56.6 2.9 slice-start
  69.6 2.9 slice-start
  72.2 1.0 slice-start.1
  82.7 2.9 slice-start
  85.2 1.0 slice-start.1
  95.8 2.9 slice-start
  98.3 1.0 slice-start.1
  108.9 2.9 slice-start
  122.0 2.9 slice-start
  135.1 2.9 slice-start
  148.2 2.9 slice-start
  150.7 1.0 slice-start.1
  161.2 2.9 slice-start
  174.3 2.9 slice-start
  187.4 2.9 slice-start
  200.5 2.9 slice-start
  213.6 2.9 slice-start
  226.7 2.9 slice-start
  229.2 1.0 slice-start.1
  239.8 2.9 slice-start
  260.4 58.2 %all-to-all-start.1 = ((bf16[128,128,128]{2,1,0:T(8,128)(2,1)}), bf16[128,128,128]{2,1,0:T(8,128)(2,1)}, u32[]{:S(2)}, u32[]{:S(2)}) async-start(bf16[128,128,128]{2,1,0:T(8,128)(2,1)} %gather_fusion.1), calls=%async_computation.1 | async-start | bytes 8388608 | tf_op jit(solution)/shard_map/all_to_all | solution.py:145
  267.9 120.6 %all-reduce.7.cloned.1.call-start = ((), (), s32[]{:S(2)}) async-start(), calls=%async_computation.2 | async-start | bytes 4194304
  325.9 4.6 %copy-start.4 = (u32[128]{0:T(128)S(1)}, u32[128]{0:T(128)}, u32[]{:S(2)}) copy-start(u32[128]{0:T(128)} %constant.81) | copy-start | bytes 1540
  (10 other events, 10.2 us)
Sparse Core Ops, SparseCore 0:
  330.7 57.7 all-reduce.6
where the time goes:
time: 404 us; the launch traced here: 401 us
  matrix products  119 us (29%)
  local copies, waits for them, and re-layouts  105 us (26%)
  waiting for transfers between devices  97.7 us (24%)
  starting transfers between devices  23.1 us (6%)
  loops' own time  22 us (5%)
  between operations  13.6 us (3%)
  other arithmetic  12.7 us (3%)
  blocking collectives  8.74 us (2%)
    convert_element_type x16, local copies, waits for them, and re-layouts, banded(): return jnp.einsum('kt,toi->koi', tap_table, selector, preferred_element_t...  52.6 us
    all_to_all x1, waiting for transfers between devices, body(): lax.all_to_all(outgoing, 'tile', split_axis=0, concat_axis=0, tiled=True)  49.9 us
    unnamed x2, waiting for transfers between devices  47.8 us
    dot_general x16, matrix products, one_group(): jnp.einsum('kobw,bkcw->boc', windows, across, preferred_element_type=jnp....  42.7 us
    dot_general x16, matrix products, one_group(): jnp.einsum('kor,rc->koc', vertical, portion, preferred_element_type=jnp.f...  40.2 us
    dot_general x17, matrix products, banded(): jnp.einsum('kt,toi->koi', tap_table, selector, preferred_element_type=jnp...  24.8 us
    another operation x1, loops' own time, match_strip(): lax.map(one_group, jnp.arange(group_total, dtype=jnp.int32))  22 us
    while x64, local copies, waits for them, and re-layouts  10.5 us
  transfers between devices with their start and end apart: 5, of which 2 were waited for; matrix products, arithmetic and copies ran while one was open for 51% of the time, Pallas kernels for 0%

commit v1 on v0

v1 whole, which is shorter than its diff:
```python
import functools

import jax
import jax.numpy as jnp
import numpy as np
from jax import lax
from jax.experimental import pallas as pl
from jax.experimental.pallas import tpu as pltpu
from jax.sharding import PartitionSpec as P

TILES_DEV = 4


HALO = 32
GROUP = 8
SPAN = 128


def halo_rows(exposure, width):
    count, length = lax.axis_size("tile"), exposure.shape[0]
    up = [(i, i + 1) for i in range(count - 1)]
    down = [(j, i) for i, j in up]
    before = lax.ppermute(exposure[length - width :], "tile", up)
    after = lax.ppermute(exposure[:width], "tile", down)
    return before, after


def wave_tables(taps, side, tall, wide, frame, skip):
    low, lanes = -(-(tall // 2 + 1) // 16) * 16, SPAN
    u, v = np.arange(low), np.arange(lanes)
    keep_u, keep_v = u <= tall // 2, v <= wide // 2
    twice_u = np.where((u == 0) | (2 * u == tall), 1.0, 2.0) * keep_u
    twice_v = np.where((v == 0) | (2 * v == wide), 1.0, 2.0) * keep_v
    turn = lambda one, other, length: 2.0 * np.pi / length * (np.outer(one, other) % length)
    place = np.arange(frame) - skip
    down = turn(u, place, tall)
    used = (place >= 0) & (place < side + taps - 1)
    rows_in = np.concatenate([np.cos(down), np.sin(down)]) * np.tile(keep_u, 2)[:, None] * used
    back = turn(np.arange(side), u, tall)
    rows_out = np.concatenate([np.cos(back) * twice_u, -np.sin(back) * twice_u], axis=1) / tall
    along = turn(np.arange(2 * side), v, wide)
    inside = (np.arange(2 * side) < wide)[:, None]
    cols_in = np.concatenate([np.cos(along), -np.sin(along)], axis=1) * inside * np.tile(keep_v, 2)
    front = turn(v, np.arange(side), wide)
    cols_out = np.concatenate([np.cos(front), -np.sin(front)]) * np.tile(twice_v, 2)[:, None] / wide
    tap_u, tap_v = turn(u, np.arange(taps), tall), turn(np.arange(taps), v, wide)
    row_taps = np.concatenate([np.cos(tap_u), np.sin(tap_u)]) * np.tile(keep_u, 2)[:, None]
    col_taps = np.concatenate([np.cos(tap_v), np.sin(tap_v)], axis=1) * np.tile(keep_v, 2)
    narrow = lambda table: jnp.asarray(table, jnp.bfloat16)
    exact = lambda table: jnp.asarray(table, jnp.float32)
    return (
        narrow(rows_in), narrow(rows_out), narrow(cols_in), narrow(cols_out),
        exact(row_taps), exact(col_taps),
    )


MESH = pl.DeviceIdType.MESH
LINE, CORES = 4, 2
PARTS = 4
WEIGHT_UNIT = 512.0


def greet(sides):
    barrier = pltpu.get_barrier_semaphore()
    for axis, count, me in sides:
        for hop in range(1, count):
            pl.semaphore_signal(
                barrier, inc=1, device_id={axis: lax.rem(me + hop, count)}, device_id_type=MESH
            )
    return barrier, sum(count - 1 for _, count, _ in sides)


def receiver(me, hop, count):
    turn = lax.rem(hop + 1, count)
    pair = turn // CORES
    dx = lax.rem(pair, LINE)
    dz = lax.rem(pair // LINE + pair, LINE)
    z, x, core = me // (LINE * CORES), lax.rem(me // CORES, LINE), lax.rem(me, CORES)
    sign = 1 - 2 * core
    z, x = lax.rem(z + sign * dz + LINE, LINE), lax.rem(x + sign * dx + LINE, LINE)
    core = lax.rem(core + turn, CORES)
    return (z * LINE + x) * CORES + core


def hop_to(owner, me, count):
    split = lambda index: (index // (LINE * CORES), index // CORES % LINE, index % CORES)
    (z, x, core), (my_z, my_x, my_core) = split(owner), split(me)
    sign = 1 - 2 * my_core
    dz, dx, dc = sign * (z - my_z) % LINE, sign * (x - my_x) % LINE, (core - my_core) % CORES
    turn = CORES * (LINE * ((dz - dx) % LINE) + dx) + dc
    return (turn + count - 1) % count


def lay_image(reach, before, exposure, after, image):
    columns = exposure.shape[1]
    tiles = 4
    wide = tiles * SPAN

    def rows(begin, width):
        return jnp.concatenate(
            [ref[:, pl.ds(begin, width)] for ref in (before, exposure, after)], axis=0
        )

    def store(number, old):
        moved = old[:, SPAN - reach : SPAN - reach + wide]
        for tile in range(tiles):
            image[number * tiles + tile] = moved[:, tile * SPAN : (tile + 1) * SPAN]

    def piece(number, carry):
        begin = pl.multiple_of(number * wide, wide)
        store(number, rows(pl.multiple_of(begin - SPAN, SPAN), wide + SPAN))
        return carry

    zeros = jnp.zeros((image.shape[1], SPAN), image.dtype)
    store(0, jnp.concatenate([zeros, rows(0, wide)], axis=1))
    lax.fori_loop(1, columns // wide, piece, 0)
    last = jnp.concatenate([rows(columns - SPAN, SPAN), zeros], axis=1)
    image[columns // SPAN] = last[:, SPAN - reach : 2 * SPAN - reach]


def match_group(
    step, order, rows_in, rows_out, cols_in, cols_out, row_wave, col_wave, coef_ref,
    image, rows_ref, cols_ref, spectrum, response, waves, warped,
):
    low, frame = rows_in.shape[0] // 2, rows_in.shape[1]
    side = warped.shape[1]
    numbers = [order[step * GROUP + q] for q in range(GROUP)]
    strips = [jnp.concatenate([image[number], image[number + 1]], axis=1) for number in numbers]
    spectrum[...] = jnp.dot(
        jnp.concatenate(strips, axis=0), cols_in[...], preferred_element_type=jnp.float32
    ).astype(jnp.bfloat16)
    scaled = [
        (row_wave[...] * coef_ref[number]).astype(jnp.bfloat16) for number in numbers
    ]
    response[...] = jnp.dot(
        jnp.concatenate(scaled, axis=0), col_wave[...], preferred_element_type=jnp.float32
    )
    for q in range(GROUP):
        both = jnp.dot(
            rows_in[...], spectrum[q * frame : (q + 1) * frame, :], preferred_element_type=jnp.float32
        )
        p_re, p_im, q_re, q_im = both[:low, :SPAN], both[:low, SPAN:], both[low:, :SPAN], both[low:, SPAN:]
        start = q * 2 * low
        a_re, a_im = response[start : start + low, :SPAN], response[start : start + low, SPAN:]
        b_re, b_im = (
            response[start + low : start + 2 * low, :SPAN],
            response[start + low : start + 2 * low, SPAN:],
        )
        even_re = p_re * a_re - p_im * a_im + q_re * b_re - q_im * b_im
        even_im = p_re * a_im + p_im * a_re + q_re * b_im + q_im * b_re
        odd_re = p_re * b_re - p_im * b_im - q_re * a_re + q_im * a_im
        odd_im = p_re * b_im + p_im * b_re - q_re * a_im - q_im * a_re
        stacked = jnp.concatenate(
            [
                jnp.concatenate([even_re, even_im], axis=1),
                jnp.concatenate([odd_re, odd_im], axis=1),
            ],
            axis=0,
        ).astype(jnp.bfloat16)
        waves[q * side : (q + 1) * side, :] = jnp.dot(
            rows_out[...], stacked, preferred_element_type=jnp.float32
        ).astype(jnp.bfloat16)
    matched = jnp.dot(waves[...], cols_out[...], preferred_element_type=jnp.float32).astype(
        jnp.bfloat16
    )
    for q in range(GROUP):
        across = jnp.dot(
            rows_ref[numbers[q]],
            matched[q * side : (q + 1) * side],
            preferred_element_type=jnp.float32,
        ).astype(jnp.bfloat16)
        warped[step * GROUP + q] = lax.dot_general(
            across,
            cols_ref[numbers[q]],
            (((1,), (1,)), ((), ())),
            preferred_element_type=jnp.float32,
        ).astype(jnp.bfloat16)


def slot_order(label_in, table_int, table_float, weight_sum, slots):
    labels = label_in[0]
    for source in range(1, label_in.shape[0]):
        labels = labels + label_in[source]
    places = labels.shape[1]
    square = (places, places)
    down, along = (lax.broadcasted_iota(jnp.int32, square, axis) for axis in (0, 1))
    slot_along = jnp.broadcast_to(labels[1:2], square)
    weight_along = jnp.broadcast_to(labels[0:1].astype(jnp.float32) / WEIGHT_UNIT, square)
    slot_down, weight_down = slot_along.T, weight_along.T
    ahead = (slot_along < slot_down) | ((slot_along == slot_down) & (along < down))
    rank = jnp.sum(ahead.astype(jnp.int32), axis=1, keepdims=True)
    chosen = rank == along
    order = jnp.sum(jnp.where(chosen, down, 0), axis=0, keepdims=True)
    slot = jnp.sum(jnp.where(chosen, slot_down, 0), axis=0, keepdims=True)
    weight = jnp.sum(jnp.where(chosen, weight_down, 0.0), axis=0, keepdims=True)
    goes_on = ((slot == pltpu.roll(slot, 1, axis=1)) & (along[:1] > 0)).astype(jnp.float32)
    up_to = jnp.sum((slot_down <= along).astype(jnp.int32), axis=0, keepdims=True)
    inside = jnp.sum((slot_down == along).astype(jnp.int32), axis=0, keepdims=True)
    last = jnp.maximum(up_to - 1, 0)
    table_int[...] = jnp.concatenate([order, last] + [order] * (table_int.shape[0] - 2), axis=0)
    table_float[...] = jnp.concatenate(
        [weight, goes_on, (inside > 0).astype(jnp.float32)] + [weight] * (table_float.shape[0] - 3),
        axis=0,
    )
    mine = jnp.where(slot_along[:slots] == down[:slots], weight_along[:slots], 0.0)
    weight_sum[...] = jnp.broadcast_to(jnp.sum(mine, axis=1, keepdims=True), (slots, places))


def coadd_kernel(
    reach, capacity, order, source, before, exposure, after, labels, rows_in, rows_out, cols_in,
    cols_out, row_wave, col_wave, coef_ref, rows_hbm, cols_hbm, coadd,
    image, spectrum, response, waves, warped, rows_ref, cols_ref,
    outgoing, label_in, table_int, table_float, weight_sum, weight_in, scale, running,
    int_smem, float_smem,
    send_sem, recv_sem, label_send, label_recv, load_sem, table_sem,
    sum_send, sum_recv, weight_send, weight_recv, *pieces,
):
    parts = len(pieces) // 3
    arrived, partial, gathered = pieces[:parts], pieces[parts : 2 * parts], pieces[2 * parts :]
    me, my_src = lax.axis_index("tile"), lax.axis_index("src")
    blocks, side = warped.shape[:2]
    count, peers = outgoing.shape[1], partial[0].shape[0]
    high = side // parts
    tiles, across = coadd.shape[0], peers
    barrier, greetings = greet((("tile", count, me), ("src", peers, my_src)))
    loads = [
        pltpu.make_async_copy(rows_hbm, rows_ref, load_sem.at[0]),
        pltpu.make_async_copy(cols_hbm, cols_ref, load_sem.at[1]),
    ]
    for load in loads:
        load.start()
    warped[...] = jnp.zeros_like(warped)
    lay_image(reach, before, exposure, after, image)
    for load in loads:
        load.wait()
    pl.semaphore_wait(barrier, greetings)

    def label_message(hop):
        return pltpu.make_async_remote_copy(
            src_ref=labels.at[hop],
            dst_ref=label_in.at[me],
            send_sem=label_send.at[hop],
            recv_sem=label_recv.at[hop],
            device_id={"tile": receiver(me, hop, count)},
            device_id_type=MESH,
        )

    def message(part, hop):
        return pltpu.make_async_remote_copy(
            src_ref=outgoing.at[part, hop],
            dst_ref=arrived[part].at[pl.ds(me * capacity, capacity)],
            send_sem=send_sem.at[part, hop],
            recv_sem=recv_sem.at[part, hop],
            device_id={"tile": receiver(me, hop, count)},
            device_id_type=MESH,
        )

    def each_hop(begin, end, act):
        def one(hop, carry):
            act(hop)
            return carry

        lax.fori_loop(begin, end, one, 0)

    def piece(hop, r, part):
        return warped[source[hop * capacity + r], part * high : (part + 1) * high, :]

    def send(part, hop):
        for r in range(capacity):
            outgoing[part, hop, r] = piece(hop, r, part)
        message(part, hop).start()

    ready = GROUP // capacity
    steps = blocks // GROUP
    each_hop(0, count - 1, lambda hop: label_message(hop).start())

    def group(step, carry):
        match_group(
            step, order, rows_in, rows_out, cols_in, cols_out, row_wave, col_wave, coef_ref,
            image, rows_ref, cols_ref, spectrum, response, waves, warped,
        )
        for hop in range(ready):
            for part in range(parts):
                send(part, step * ready + hop)
        return carry

    lax.fori_loop(0, steps, group, 0)
    for part in range(parts):
        each_hop(steps * ready, count - 1, lambda hop, part=part: send(part, hop))
        for r in range(capacity):
            arrived[part][me * capacity + r] = piece(count - 1, r, part)

    label_in[me] = labels[count - 1]
    each_hop(0, count - 1, lambda hop: label_message(hop).wait())
    slot_order(label_in, table_int, table_float, weight_sum, tiles * across * across)
    moves = [
        pltpu.make_async_copy(table_int, int_smem, table_sem.at[0]),
        pltpu.make_async_copy(table_float, float_smem, table_sem.at[1]),
    ]
    for move in moves:
        move.start()

    def to_peer(hop, from_ref, to_ref, send_sem, recv_sem):
        return pltpu.make_async_remote_copy(
            src_ref=from_ref,
            dst_ref=to_ref,
            send_sem=send_sem,
            recv_sem=recv_sem,
            device_id={"src": lax.rem(my_src + hop, peers)},
            device_id_type=MESH,
        )

    def weight_message(hop):
        return to_peer(
            hop, weight_sum, weight_in.at[hop - 1], weight_send.at[hop - 1], weight_recv.at[hop - 1]
        )

    def sum_message(part, hop):
        return to_peer(
            hop,
            partial[part].at[lax.rem(my_src + hop, peers)],
            gathered[part].at[hop - 1],
            sum_send.at[part, hop - 1],
            sum_recv.at[part, hop - 1],
        )

    for hop in range(1, peers):
        weight_message(hop).start()
    for move in moves:
        move.wait()

    def stack(part):
        def add(place, total):
            block = arrived[part][int_smem[0, place]].astype(jnp.float32)
            total = total * float_smem[1, place] + float_smem[0, place] * block
            running[place] = total
            return total

        lax.fori_loop(
            0, arrived[part].shape[0], add, jnp.zeros((high, side), jnp.float32), unroll=4
        )

        def take(slot, carry):
            row = lax.rem(slot // across, across)
            place = slot // (across * across) * across + lax.rem(slot, across)
            total = running[int_smem[1, slot]] * float_smem[2, slot]
            partial[part][row, place] = total.astype(jnp.bfloat16)
            return carry

        lax.fori_loop(0, tiles * across * across, take, 0, unroll=4)

    def finish(part):
        for hop in range(1, peers):
            sum_message(part, hop).wait()
        for tile in range(tiles):
            for column in range(across):
                place = tile * across + column
                total = partial[part][my_src, place].astype(jnp.float32)
                for hop in range(peers - 1):
                    total = total + gathered[part][hop, place].astype(jnp.float32)
                slot = (tile * across + my_src) * across + column
                coadd[
                    tile, part * high : (part + 1) * high, column * side : (column + 1) * side
                ] = total * scale[slot]

    for part in range(parts):
        each_hop(0, count - 1, lambda hop, part=part: message(part, hop).wait_recv())
        stack(part)
        for hop in range(1, peers):
            sum_message(part, hop).start()
        if part == 0:
            for hop in range(1, peers):
                weight_message(hop).wait()
            weight = weight_sum[...]
            for hop in range(peers - 1):
                weight = weight + weight_in[hop]
            factor = 1.0 / jnp.maximum(weight, 1.0)
            for slot in range(scale.shape[0]):
                scale[slot] = factor[slot : slot + 1]
        else:
            finish(part - 1)
    finish(parts - 1)
    for part in range(parts):
        each_hop(0, count - 1, lambda hop, part=part: message(part, hop).wait_send())


def coadd_tiles(
    exposure, row_bases, col_bases, coefficients, warp_rows, warp_cols, order, source, labels, capacity
):
    before, after = halo_rows(exposure, HALO)
    blocks, side = warp_rows.shape[:2]
    count, tall_label, places = labels.shape
    peers = lax.axis_size("src")
    slots = TILES_DEV * peers * peers
    basis_count, taps = row_bases.shape
    columns = exposure.shape[1]
    reach = taps // 2
    frame = side + 2 * HALO
    tall = -(-(side + taps - 1) // 16) * 16
    rows_in, rows_out, cols_in, cols_out, row_taps, col_taps = wave_tables(
        taps, side, tall, side + taps - 1, frame, HALO - reach
    )
    spare = SPAN - basis_count
    exact = lax.Precision.HIGHEST
    row_wave = jnp.dot(
        row_taps, jnp.pad(row_bases.astype(jnp.float32).T, ((0, 0), (0, spare))), precision=exact
    )
    col_wave = jnp.dot(
        jnp.pad(col_bases.astype(jnp.float32), ((0, spare), (0, 0))), col_taps, precision=exact
    ).astype(jnp.bfloat16)
    padded_coefficients = jnp.pad(coefficients, ((0, 0), (0, spare)))[:, None, :]
    near, far = pl.BlockSpec(memory_space=pltpu.VMEM), pl.BlockSpec(memory_space=pl.ANY)
    table = pl.BlockSpec(memory_space=pltpu.SMEM)
    high = side // PARTS
    per = slots // peers
    narrow, dma = jnp.bfloat16, pltpu.SemaphoreType.DMA
    return pl.pallas_call(
        functools.partial(coadd_kernel, reach, capacity),
        in_specs=[table, table] + [near] * 11 + [far, far],
        out_specs=near,
        out_shape=jax.ShapeDtypeStruct((TILES_DEV, side, peers * side), jnp.float32),
        scratch_shapes=[
            pltpu.VMEM((columns // SPAN + 1, frame, SPAN), narrow),
            pltpu.VMEM((GROUP * frame, 2 * SPAN), narrow),
            pltpu.VMEM((GROUP * rows_in.shape[0], 2 * SPAN), jnp.float32),
            pltpu.VMEM((GROUP * side, 2 * SPAN), narrow),
            pltpu.VMEM((blocks, side, side), narrow),
            pltpu.VMEM((blocks, side, side), narrow),
            pltpu.VMEM((blocks, side, side), narrow),
            pltpu.VMEM((PARTS, count, capacity, high, side), narrow),
            pltpu.VMEM(labels.shape, jnp.int32),
            pltpu.VMEM((tall_label, places), jnp.int32),
            pltpu.VMEM((tall_label, places), jnp.float32),
            pltpu.VMEM((slots, places), jnp.float32),
            pltpu.VMEM((peers - 1, slots, places), jnp.float32),
            pltpu.VMEM((slots, 1, places), jnp.float32),
            pltpu.VMEM((count * capacity, high, side), jnp.float32),
            pltpu.SMEM((tall_label, places), jnp.int32),
            pltpu.SMEM((tall_label, places), jnp.float32),
            dma((PARTS, count)),
            dma((PARTS, count)),
            dma((count,)),
            dma((count,)),
            dma((2,)),
            dma((2,)),
            dma((PARTS, peers - 1)),
            dma((PARTS, peers - 1)),
            dma((peers - 1,)),
            dma((peers - 1,)),
            *[pltpu.VMEM((count * capacity, high, side), narrow) for _ in range(PARTS)],
            *[pltpu.VMEM((peers, per, high, side), narrow) for _ in range(PARTS)],
            *[pltpu.VMEM((peers - 1, per, high, side), narrow) for _ in range(PARTS)],
        ],
        compiler_params=pltpu.CompilerParams(
            collective_id=0, has_side_effects=True, vmem_limit_bytes=50 * 1024 * 1024
        ),
        cost_estimate=pl.CostEstimate(flops=4 << 30, bytes_accessed=10 << 20, transcendentals=0),
    )(
        order, source, before, exposure, after, labels, rows_in, rows_out, cols_in, cols_out,
        row_wave, col_wave, padded_coefficients, warp_rows, warp_cols,
    )


def route(owner, count, capacity):
    blocks = owner.shape[0]
    hop = hop_to(owner, lax.axis_index("tile"), count)
    square = (blocks, blocks)
    number = lax.broadcasted_iota(jnp.int32, square, 1)
    earlier = number < lax.broadcasted_iota(jnp.int32, square, 0)
    same, before = hop[:, None] == hop[None, :], hop[None, :] < hop[:, None]
    rank = jnp.sum((same & earlier).astype(jnp.int32), axis=1)
    position = rank + jnp.sum(before.astype(jnp.int32), axis=1)
    order = jnp.sum(
        jnp.where(lax.broadcasted_iota(jnp.int32, square, 0) == position[None, :], number, 0), axis=1
    )
    place = hop * capacity + rank
    found = lax.broadcasted_iota(jnp.int32, (count * capacity, blocks), 0) == place[None, :]
    source = jnp.sum(jnp.where(found, position[None, :], 0), axis=1)
    return order, source, found


def body(
    exposure,
    row_bases,
    col_bases,
    coefficients,
    warp_rows,
    warp_cols,
    variance,
    footprint,
    slot_index,
):
    count = lax.axis_size("tile")
    blocks = warp_rows.shape[2]
    capacity = max(2, 2 * blocks // count)
    order, source, found = route(footprint[0, 0, :, 0], count, capacity)
    weight = (1.0 / variance[0, 0]).astype(jnp.bfloat16).astype(jnp.float32)
    units = (weight * WEIGHT_UNIT).astype(jnp.int32)
    fields = [
        jnp.sum(jnp.where(found, values[None, :], 0), axis=1).reshape(count, capacity)
        for values in (units, slot_index[0, 0])
    ]
    labels = jnp.stack([jnp.tile(field, (1, count)) for field in fields], axis=1)
    mine = lax.broadcasted_iota(jnp.int32, labels.shape, 2) // capacity == lax.axis_index("tile")
    labels = jnp.pad(jnp.where(mine, labels, 0), ((0, 0), (0, 6), (0, 0)))
    return coadd_tiles(
        exposure[0], row_bases, col_bases, coefficients[0, 0], warp_rows[0, 0], warp_cols[0, 0],
        order, source, labels, capacity,
    )


def solution(mesh):
    placed = (
        P("src", "tile", None),
        P(),
        P(),
        P("src", "tile", None, None),
        P("src", "tile", None, None, None),
        P("src", "tile", None, None, None),
        P("src", "tile", None),
        P("src", "tile", None, None),
        P("src", "tile", None),
    )
    return jax.shard_map(
        body, mesh=mesh, in_specs=placed, out_specs=P("tile", "src", None), check_vma=False
    )
```

time: 404 us -> 104 us (0.26)
  matrix products: 119 us -> 0.38 us
  local copies, waits for them, and re-layouts: 105 us -> 3.12 us
  waiting for transfers between devices: 97.7 us -> 4.3 us
  Pallas kernels: 0 us -> 88.9 us
  loops' own time: 22 us -> 0 us
  starting transfers between devices: 23.1 us -> 5.6 us
  between operations: 13.6 us -> 0.33 us
  other arithmetic: 12.7 us -> 0.57 us
  blocking collectives: 8.74 us -> 0 us
    dot_general x51 -> x2, matrix products: 119 us -> 0.38 us  [the longest x1 0.19 us: coadd_tiles(): jnp.dot(jnp.pad(col_bases.astype(jnp.float32), ((0, spare), (0, 0))), col...]
    pallas_call x0 -> x1, Pallas kernels: none -> 88.9 us  [coadd_tiles(): pl.pallas_call(functools.partial(coadd_kernel, reach, capacity), in_specs...]
    convert_element_type x18 -> x0, local copies, waits for them, and re-layouts: 52.7 us -> none  [the longest x16 52.6 us: banded(): return jnp.einsum('kt,toi->koi', tap_table, selector, preferred_element_t...]
    all_to_all x2 -> x0, waiting for transfers between devices: 49.9 us -> none  [the longest x1 49.9 us: body(): lax.all_to_all(outgoing, 'tile', split_axis=0, concat_axis=0, tiled=True)]
    unnamed x2 -> x0, waiting for transfers between devices: 47.8 us -> none
    another operation x1 -> x0, loops' own time: 22 us -> none  [match_strip(): lax.map(one_group, jnp.arange(group_total, dtype=jnp.int32))]
    all_to_all x2 -> x0, starting transfers between devices: 17.4 us -> none  [the longest x1 9.91 us: body(): lax.all_to_all(metadata, 'tile', split_axis=0, concat_axis=0, tiled=True)]
    while x66 -> x0, local copies, waits for them, and re-layouts: 11.1 us -> none
  transfers between devices with their start and end apart: 5 -> 2, of which waited for: 2 -> 2; matrix products, arithmetic and copies ran while one was open for 51% -> 2% of each run, Pallas kernels for 0% -> 0%
where the time goes in v1:
time: 104 us; the launch traced here: 103 us
  Pallas kernels  88.9 us (85%)
  starting transfers between devices  5.6 us (5%)
  waiting for transfers between devices  4.3 us (4%)
  local copies, waits for them, and re-layouts  3.12 us (3%)
    pallas_call x1, Pallas kernels, coadd_tiles(): pl.pallas_call(functools.partial(coadd_kernel, reach, capacity), in_specs...  88.9 us
    ppermute x1, waiting for transfers between devices, halo_rows(): after = lax.ppermute(exposure[:width], 'tile', down)  3.41 us
    ppermute x1, starting transfers between devices, halo_rows(): before = lax.ppermute(exposure[length - width:], 'tile', up)  3.02 us
    ppermute x1, starting transfers between devices, halo_rows(): after = lax.ppermute(exposure[:width], 'tile', down)  2.58 us
  transfers between devices with their start and end apart: 2, of which 2 were waited for; matrix products, arithmetic and copies ran while one was open for 2% of the time, Pallas kernels for 0%

profile of v1, /device:TPU:3, one launch (start us, length us, event | category | flops | bytes accessed | tf_op | source)
XLA Modules:
  0.0 103.2 jit_solution(17986545887087278895)
XLA Ops:
  0.0 0.0 copy-start
  0.0 0.0 copy-start.3
  0.0 0.0 copy-start.1
  0.0 0.0 copy-start.11
  0.1 0.0 copy-start.9
  0.1 0.0 copy-start.10
  0.1 0.0 copy-start.6
  0.1 0.0 copy-start.8
  0.1 1.5 %slice_bitcast_fusion = (bf16[32,8192]{1,0:T(8,128)(2,1)S(1)}, bf16[32,8192]{1,0:T(8,128)(2,1)S(1)}) fusion(bf16[1,128,8192]{2,1,0:T(8,128)(2,1)} %param.15), kind=kLoop, calls=%fused_computation.1 | loop fusion | bytes 2097152 | tf_op jit(solution)/shard_map/slice | solution.py:24
  1.6 2.6 %collective-permute-start.1 = (bf16[32,8192]{1,0:T(8,128)(2,1)S(1)}, bf16[32,8192]{1,0:T(8,128)(2,1)S(1)}, u32[]{:S(2)}, u32[]{:S(2)}) collective-permute-start(bf16[32,8192]{1,0:T(8,128)(2,1)S(1)} %get-tuple-element.10), channel_id=1, source_target_pairs={{1,0},{2,1},{3,2},{4,3},{5,4},{6,5},{7,6},{8,7},{9,8},{10,9},{11,1... | collective-permute-start | bytes 1572872 | tf_op jit(solution)/shard_map/ppermute | solution.py:24
  4.2 3.0 %collective-permute-start = (bf16[32,8192]{1,0:T(8,128)(2,1)S(1)}, bf16[32,8192]{1,0:T(8,128)(2,1)S(1)}, u32[]{:S(2)}, u32[]{:S(2)}) collective-permute-start(bf16[32,8192]{1,0:T(8,128)(2,1)S(1)} %get-tuple-element.11), channel_id=1, source_target_pairs={{0,1},{1,2},{2,3},{3,4},{4,5},{5,6},{6,7},{7,8},{8,9},{9,10},{10,1... | collective-permute-start | bytes 1572872 | tf_op jit(solution)/shard_map/ppermute | solution.py:23
  7.3 0.0 copy-done.11
  7.4 0.2 convert_reduce_fusion
  7.6 0.1 multiply_add_fusion
  7.6 0.1 select_reduce_fusion.1
  7.7 0.1 tile.18
  7.8 0.1 copy.22
  7.9 0.1 tile.21
  8.0 0.1 copy.23
  8.1 0.1 copy.26
  8.2 0.1 copy.25
  8.3 0.1 copy.24
  8.4 0.1 compare_select_fusion
  8.5 0.1 select_reduce_fusion.3.order
  8.6 0.2 convolution_convert_fusion.col_wave
  8.8 0.2 fusion.1.row_wave
  9.0 3.4 %collective-permute-done.1.after = bf16[32,8192]{1,0:T(8,128)(2,1)S(1)} collective-permute-done((bf16[32,8192]{1,0:T(8,128)(2,1)S(1)}, bf16[32,8192]{1,0:T(8,128)(2,1)S(1)}, u32[]{:S(2)}, u32[]{:S(2)}) %collective-permute-start.1) | collective-permute-done | bytes 524320 | tf_op jit(solution)/shard_map/ppermute | solution.py:24
  12.4 0.9 collective-permute-done.before
  13.3 0.0 copy-done.2
  13.3 0.0 copy-done.3
  13.3 88.9 %shard_map.145 = f32[4,128,512]{2,1,0:T(8,128)S(1)} custom-call(s32[64]{0:T(128)S(1)} %select_reduce_fusion.3.order, s32[128]{0:T(128)S(1)} %get-tuple-element.7.source, bf16[32,8192]{1,0:T(8,128)(2,1)S(1)} %collective-permute-done.before, bf16[128,8192]{1,0:T(8,128)(2,1)} %bitcast.38, bf16[32,8192]{1,0:T(8,128)(2,1)S(1)} %collective-permute-done.1.after, ...), custom_call_target="tpu_custom_call" | custom-call | flops 4294967296 | bytes 10485760 | tf_op jit(solution)/shard_map/pallas_call | solution.py:417
  102.3 1.0 copy.28
  (21 shorter events, 0.2 us)
Async XLA Ops:
  0.0 8.6 %copy-start.5 = (f32[41,256]{1,0:T(8,128)S(1)}, f32[41,256]{1,0:T(8,128)}, u32[]{:S(2)}) copy-start(f32[41,256]{1,0:T(8,128)} %constant.170.clone) | copy-start | bytes 125956
  0.0 8.8 %copy-start.4 = (f32[192,41]{1,0:T(8,128)S(1)}, f32[192,41]{1,0:T(8,128)}, u32[]{:S(2)}) copy-start(f32[192,41]{1,0:T(8,128)} %constant.169.clone) | copy-start | bytes 94468
  0.0 13.3 %copy-start.2 = (bf16[256,128]{1,0:T(8,128)(2,1)S(1)}, bf16[256,128]{1,0:T(8,128)(2,1)}, u32[]{:S(2)}) copy-start(bf16[256,128]{1,0:T(8,128)(2,1)} %constant.168.clone.cols_out) | copy-start | bytes 196612
  0.0 13.3 %copy-start = (bf16[256,256]{1,0:T(8,128)(2,1)S(1)}, bf16[256,256]{1,0:T(8,128)(2,1)}, u32[]{:S(2)}) copy-start(bf16[256,256]{1,0:T(8,128)(2,1)} %constant.167.clone.cols_in) | copy-start | bytes 393220
  0.0 13.3 %copy-start.3 = (bf16[128,192]{1,0:T(8,128)(2,1)S(1)}, bf16[128,192]{1,0:T(8,128)(2,1)}, u32[]{:S(2)}) copy-start(bf16[128,192]{1,0:T(8,128)(2,1)} %constant.166.clone.rows_out) | copy-start | bytes 147460
  0.0 13.3 %copy-start.1 = (bf16[192,192]{1,0:T(8,128)(2,1)S(1)}, bf16[192,192]{1,0:T(8,128)(2,1)}, u32[]{:S(2)}) copy-start(bf16[192,192]{1,0:T(8,128)(2,1)} %constant.165.clone.rows_in) | copy-start | bytes 221188
  0.0 7.2 %copy-start.11 = (f32[1,1,64]{2,1,0:T(1,128)S(1)}, f32[1,1,64]{2,1,0:T(1,128)}, u32[]{:S(2)}) copy-start(f32[1,1,64]{2,1,0:T(1,128)} %param.21) | copy-start | bytes 772
  0.1 7.3 %copy-start.9 = (s32[1,1,64,1]{2,3,1,0:T(1,128)S(1)}, s32[1,1,64,1]{2,3,1,0:T(1,128)}, u32[]{:S(2)}) copy-start(s32[1,1,64,1]{2,3,1,0:T(1,128)} %param.22) | copy-start | bytes 772
  0.1 7.5 %copy-start.10 = (s32[1,1,64]{2,1,0:T(1,128)S(1)}, s32[1,1,64]{2,1,0:T(1,128)}, u32[]{:S(2)}) copy-start(s32[1,1,64]{2,1,0:T(1,128)} %param.23) | copy-start | bytes 772
  0.1 8.0 %copy-start.6 = (f32[1,1,64,27]{2,1,3,0:T(1,128)S(1)}, f32[1,1,64,27]{2,1,3,0:T(1,128)}, u32[]{:S(2)}) copy-start(f32[1,1,64,27]{2,1,3,0:T(1,128)} %param.18) | copy-start | bytes 20740
  0.1 8.5 %copy-start.8 = (bf16[27,41]{1,0:T(8,128)(2,1)S(1)}, bf16[27,41]{1,0:T(8,128)(2,1)}, u32[]{:S(2)}) copy-start(bf16[27,41]{1,0:T(8,128)(2,1)} %param.17) | copy-start | bytes 6646
  0.1 8.7 %copy-start.7 = (bf16[27,41]{1,0:T(8,128)(2,1)S(1)}, bf16[27,41]{1,0:T(8,128)(2,1)}, u32[]{:S(2)}) copy-start(bf16[27,41]{1,0:T(8,128)(2,1)} %param.16) | copy-start | bytes 6646
  1.6 10.8 %collective-permute-start.1 = (bf16[32,8192]{1,0:T(8,128)(2,1)S(1)}, bf16[32,8192]{1,0:T(8,128)(2,1)S(1)}, u32[]{:S(2)}, u32[]{:S(2)}) collective-permute-start(bf16[32,8192]{1,0:T(8,128)(2,1)S(1)} %get-tuple-element.10), channel_id=1, source_target_pairs={{1,0},{2,1},{3,2},{4,3},{5,4},{6,5},{7,6},{8,7},{9,8},{10,9},{11,1... | collective-permute-start | bytes 1572872 | tf_op jit(solution)/shard_map/ppermute | solution.py:24
  4.2 9.1 %collective-permute-start = (bf16[32,8192]{1,0:T(8,128)(2,1)S(1)}, bf16[32,8192]{1,0:T(8,128)(2,1)S(1)}, u32[]{:S(2)}, u32[]{:S(2)}) collective-permute-start(bf16[32,8192]{1,0:T(8,128)(2,1)S(1)} %get-tuple-element.11), channel_id=1, source_target_pairs={{0,1},{1,2},{2,3},{3,4},{4,5},{5,6},{6,7},{7,8},{8,9},{9,10},{10,1... | collective-permute-start | bytes 1572872 | tf_op jit(solution)/shard_map/ppermute | solution.py:23

commit v2 on v1

v2 whole, which is shorter than its diff:
```python
import functools

import jax
import jax.numpy as jnp
import numpy as np
from jax import lax
from jax.experimental import pallas as pl
from jax.experimental.pallas import tpu as pltpu
from jax.sharding import PartitionSpec as P

TILES_DEV = 4


HALO = 32
GROUP = 8
SPAN = 128


def wave_tables(taps, side, tall, wide, frame, skip):
    low, lanes = -(-(tall // 2 + 1) // 16) * 16, SPAN
    u, v = np.arange(low), np.arange(lanes)
    keep_u, keep_v = u <= tall // 2, v <= wide // 2
    twice_u = np.where((u == 0) | (2 * u == tall), 1.0, 2.0) * keep_u
    twice_v = np.where((v == 0) | (2 * v == wide), 1.0, 2.0) * keep_v
    turn = lambda one, other, length: 2.0 * np.pi / length * (np.outer(one, other) % length)
    place = np.arange(frame) - skip
    down = turn(u, place, tall)
    used = (place >= 0) & (place < side + taps - 1)
    rows_in = np.concatenate([np.cos(down), np.sin(down)]) * np.tile(keep_u, 2)[:, None] * used
    back = turn(np.arange(side), u, tall)
    rows_out = np.concatenate([np.cos(back) * twice_u, -np.sin(back) * twice_u], axis=1) / tall
    along = turn(np.arange(2 * side), v, wide)
    inside = (np.arange(2 * side) < wide)[:, None]
    cols_in = np.concatenate([np.cos(along), -np.sin(along)], axis=1) * inside * np.tile(keep_v, 2)
    front = turn(v, np.arange(side), wide)
    cols_out = np.concatenate([np.cos(front), -np.sin(front)]) * np.tile(twice_v, 2)[:, None] / wide
    tap_u, tap_v = turn(u, np.arange(taps), tall), turn(np.arange(taps), v, wide)
    row_taps = np.concatenate([np.cos(tap_u), np.sin(tap_u)]) * np.tile(keep_u, 2)[:, None]
    col_taps = np.concatenate([np.cos(tap_v), np.sin(tap_v)], axis=1) * np.tile(keep_v, 2)
    places, rows = [], []
    for table in (rows_in, rows_out, cols_in, cols_out, row_taps, col_taps):
        places.append((sum(part.shape[0] for part in rows), *table.shape))
        rows.append(np.pad(table, ((0, -table.shape[0] % 16), (0, 2 * side - table.shape[1]))))
    return jnp.asarray(np.concatenate(rows), jnp.float32), places


MESH = pl.DeviceIdType.MESH
LINE, CORES = 4, 2
PARTS = 4
WEIGHT_UNIT = 512.0


def greet(sides):
    barrier = pltpu.get_barrier_semaphore()
    for axis, count, me in sides:
        for hop in range(1, count):
            pl.semaphore_signal(
                barrier, inc=1, device_id={axis: lax.rem(me + hop, count)}, device_id_type=MESH
            )
    return barrier, sum(count - 1 for _, count, _ in sides)


def receiver(me, hop, count):
    turn = lax.rem(hop + 1, count)
    pair = turn // CORES
    dx = lax.rem(pair, LINE)
    dz = lax.rem(pair // LINE + pair, LINE)
    z, x, core = me // (LINE * CORES), lax.rem(me // CORES, LINE), lax.rem(me, CORES)
    sign = 1 - 2 * core
    z, x = lax.rem(z + sign * dz + LINE, LINE), lax.rem(x + sign * dx + LINE, LINE)
    core = lax.rem(core + turn, CORES)
    return (z * LINE + x) * CORES + core


def hop_to(owner, me):
    wide, line = LINE * CORES, LINE - 1
    sign = 1 - 2 * lax.rem(me, CORES)
    dz = (sign * (owner // wide - me // wide)) & line
    dx = (sign * (((owner // CORES) & line) - lax.rem(me // CORES, LINE))) & line
    dc = (owner - me) & (CORES - 1)
    turn = CORES * (LINE * ((dz - dx) & line) + dx) + dc
    return (turn - 1) & (LINE * wide - 1)


def route(me, capacity, owner_ref, slot_ref, variance_ref, route_table, fields):
    blocks, places = owner_ref.shape[1], route_table.shape[1]
    square = (blocks, blocks)
    down, along = (lax.broadcasted_iota(jnp.int32, square, axis) for axis in (0, 1))
    hop_along = jnp.broadcast_to(hop_to(owner_ref[...], me), square)
    hop_down = hop_along.T
    count = lambda mask: jnp.sum(mask.astype(jnp.int32), axis=1, keepdims=True)
    rank = count((hop_along == hop_down) & (along < down))
    position = rank + count(hop_along < hop_down)
    weight = (1.0 / variance_ref[...]).astype(jnp.bfloat16).astype(jnp.float32)
    units = (jnp.broadcast_to(weight, square).T * WEIGHT_UNIT).astype(jnp.int32)[:, :1]
    slot = jnp.broadcast_to(slot_ref[...], square).T[:, :1]
    table = (blocks, places)
    number = lax.broadcasted_iota(jnp.int32, table, 0)
    lane = lax.broadcasted_iota(jnp.int32, table, 1)
    found = lane == hop_down[:, :1] * capacity + rank
    pick = lambda mask, values: jnp.sum(jnp.where(mask, values, 0), axis=0, keepdims=True)
    order = pick(lane == position, number)
    source = pick(found, position)
    route_table[...] = jnp.concatenate([order, source] + [order] * (route_table.shape[0] - 2), axis=0)
    row = [pick(found, units), pick(found, slot)]
    fields[...] = jnp.concatenate(row + [jnp.zeros_like(row[0])] * (fields.shape[0] - 2), axis=0)


def transform_rows(reach, rows_in, before, exposure, after, strip):
    columns = exposure.shape[1]
    tiles = 4
    wide = tiles * SPAN

    def rows(begin, width):
        return jnp.concatenate(
            [ref[:, pl.ds(begin, width)] for ref in (before, exposure, after)], axis=0
        )

    def spectra(window):
        return jnp.dot(rows_in[...], window, preferred_element_type=jnp.float32).astype(strip.dtype)

    def store(number, old):
        moved = spectra(old[:, SPAN - reach : SPAN - reach + wide])
        for tile in range(tiles):
            strip[number * tiles + tile] = moved[:, tile * SPAN : (tile + 1) * SPAN]

    def piece(number, carry):
        begin = pl.multiple_of(number * wide, wide)
        store(number, rows(pl.multiple_of(begin - SPAN, SPAN), wide + SPAN))
        return carry

    zeros = jnp.zeros((rows_in.shape[1], SPAN), exposure.dtype)
    store(0, jnp.concatenate([zeros, rows(0, wide)], axis=1))
    lax.fori_loop(1, columns // wide, piece, 0)
    last = jnp.concatenate([rows(columns - SPAN, SPAN), zeros], axis=1)
    strip[columns // SPAN] = spectra(last[:, SPAN - reach : 2 * SPAN - reach])


def match_group(
    step, route_smem, rows_out, cols_in, cols_out, row_wave, col_wave, coef_ref,
    strip, rows_ref, cols_ref, spectrum, response, warps, waves, warped,
):
    low = row_wave.shape[0] // 2
    side = warped.shape[1]
    numbers = [route_smem[0, step * GROUP + q] for q in range(GROUP)]
    windows = [jnp.concatenate([strip[number], strip[number + 1]], axis=1) for number in numbers]
    spectrum[...] = jnp.dot(
        jnp.concatenate(windows, axis=0), cols_in[...], preferred_element_type=jnp.float32
    )
    scaled = [(row_wave[...] * coef_ref[number]).astype(jnp.bfloat16) for number in numbers]
    response[...] = jnp.dot(
        jnp.concatenate(scaled, axis=0), col_wave[...], preferred_element_type=jnp.float32
    )
    warps[...] = jnp.dot(
        jnp.concatenate([rows_ref[number] for number in numbers], axis=0),
        rows_out[...],
        preferred_element_type=jnp.float32,
    ).astype(jnp.bfloat16)
    for q in range(GROUP):
        top = slice(q * 2 * low, q * 2 * low + low)
        end = slice(q * 2 * low + low, (q + 1) * 2 * low)
        p_re, p_im = spectrum[top, :SPAN], spectrum[top, SPAN:]
        q_re, q_im = spectrum[end, :SPAN], spectrum[end, SPAN:]
        a_re, a_im = response[top, :SPAN], response[top, SPAN:]
        b_re, b_im = response[end, :SPAN], response[end, SPAN:]
        even_re = p_re * a_re - p_im * a_im + q_re * b_re - q_im * b_im
        even_im = p_re * a_im + p_im * a_re + q_re * b_im + q_im * b_re
        odd_re = p_re * b_re - p_im * b_im - q_re * a_re + q_im * a_im
        odd_im = p_re * b_im + p_im * b_re - q_re * a_im - q_im * a_re
        stacked = jnp.concatenate(
            [
                jnp.concatenate([even_re, even_im], axis=1),
                jnp.concatenate([odd_re, odd_im], axis=1),
            ],
            axis=0,
        ).astype(jnp.bfloat16)
        waves[q * side : (q + 1) * side, :] = jnp.dot(
            warps[q * side : (q + 1) * side, :], stacked, preferred_element_type=jnp.float32
        ).astype(jnp.bfloat16)
    across = jnp.dot(waves[...], cols_out[...], preferred_element_type=jnp.float32).astype(
        jnp.bfloat16
    )
    for q in range(GROUP):
        warped[step * GROUP + q] = lax.dot_general(
            across[q * side : (q + 1) * side],
            cols_ref[numbers[q]],
            (((1,), (1,)), ((), ())),
            preferred_element_type=jnp.float32,
        ).astype(jnp.bfloat16)


def slot_order(label_in, table_int, table_float, weight_sum, slots):
    labels = label_in[0]
    for source in range(1, label_in.shape[0]):
        labels = labels + label_in[source]
    places = labels.shape[1]
    square = (places, places)
    down, along = (lax.broadcasted_iota(jnp.int32, square, axis) for axis in (0, 1))
    slot_along = jnp.broadcast_to(labels[1:2], square)
    weight_along = jnp.broadcast_to(labels[0:1].astype(jnp.float32) / WEIGHT_UNIT, square)
    slot_down, weight_down = slot_along.T, weight_along.T
    ahead = (slot_along < slot_down) | ((slot_along == slot_down) & (along < down))
    rank = jnp.sum(ahead.astype(jnp.int32), axis=1, keepdims=True)
    chosen = rank == along
    order = jnp.sum(jnp.where(chosen, down, 0), axis=0, keepdims=True)
    slot = jnp.sum(jnp.where(chosen, slot_down, 0), axis=0, keepdims=True)
    weight = jnp.sum(jnp.where(chosen, weight_down, 0.0), axis=0, keepdims=True)
    goes_on = ((slot == pltpu.roll(slot, 1, axis=1)) & (along[:1] > 0)).astype(jnp.float32)
    up_to = jnp.sum((slot_down <= along).astype(jnp.int32), axis=0, keepdims=True)
    inside = jnp.sum((slot_down == along).astype(jnp.int32), axis=0, keepdims=True)
    last = jnp.maximum(up_to - 1, 0)
    table_int[...] = jnp.concatenate([order, last] + [order] * (table_int.shape[0] - 2), axis=0)
    table_float[...] = jnp.concatenate(
        [weight, goes_on, (inside > 0).astype(jnp.float32)] + [weight] * (table_float.shape[0] - 3),
        axis=0,
    )
    mine = jnp.where(slot_along[:slots] == down[:slots], weight_along[:slots], 0.0)
    weight_sum[...] = jnp.broadcast_to(jnp.sum(mine, axis=1, keepdims=True), (slots, places))


def coadd_kernel(
    reach, capacity, places, exposure_hbm, rows_hbm, cols_hbm, tables_hbm,
    row_bases, col_bases, coefficients, variance, owner, slot_index, coadd,
    exposure, before, after, strip, tables, wave_table, row_wave, col_wave, coef_ref,
    route_table, fields, labels,
    spectrum, response, warps, waves, warped, rows_ref, cols_ref,
    outgoing, label_in, table_int, table_float, weight_sum, weight_in, scale, running,
    route_smem, int_smem, float_smem,
    halo_send, halo_recv, send_sem, recv_sem, label_send, label_recv, load_sem, table_sem,
    sum_send, sum_recv, weight_send, weight_recv, *pieces,
):
    parts = len(pieces) // 3
    arrived, partial, gathered = pieces[:parts], pieces[parts : 2 * parts], pieces[2 * parts :]
    me, my_src = lax.axis_index("tile"), lax.axis_index("src")
    blocks, side = warped.shape[:2]
    count, peers = outgoing.shape[1], partial[0].shape[0]
    high = side // parts
    tiles, across = coadd.shape[0], peers
    barrier, greetings = greet((("tile", count, me), ("src", peers, my_src)))
    loads = [
        pltpu.make_async_copy(from_ref, to_ref, load_sem.at[number])
        for number, (from_ref, to_ref) in enumerate(
            (
                (tables_hbm, wave_table),
                (exposure_hbm, exposure),
                (rows_hbm, rows_ref),
                (cols_hbm, cols_ref),
            )
        )
    ]
    for load in loads:
        load.start()
    route(me, capacity, owner, slot_index, variance, route_table, fields)
    move = pltpu.make_async_copy(route_table, route_smem, table_sem.at[0])
    move.start()
    by_block = jnp.concatenate([coefficients[k] for k in range(coefficients.shape[0])], axis=0).T
    for number in range(blocks):
        coef_ref[number] = by_block[number : number + 1, :]
    lane = lax.broadcasted_iota(jnp.int32, fields.shape, 1)
    for hop in range(count):
        moved = pltpu.roll(
            fields[...], lax.rem((me - hop + count) * capacity, lane.shape[1]), axis=1
        )
        labels[hop] = jnp.where(lane // capacity == me, moved, 0)
    pl.semaphore_wait(barrier, greetings)

    def halo(number, begin, to_ref, neighbour):
        return pltpu.make_async_remote_copy(
            src_ref=exposure_hbm.at[pl.ds(begin, HALO)],
            dst_ref=to_ref,
            send_sem=halo_send.at[number],
            recv_sem=halo_recv.at[number],
            device_id={"tile": neighbour},
            device_id_type=MESH,
        )

    down = halo(0, side - HALO, before, lax.rem(me + 1, count))
    up = halo(1, 0, after, lax.rem(me + count - 1, count))

    @pl.when(me < count - 1)
    def _():
        down.start()

    @pl.when(me > 0)
    def _():
        up.start()

    @pl.when(me == 0)
    def _():
        before[...] = jnp.zeros_like(before)

    @pl.when(me == count - 1)
    def _():
        after[...] = jnp.zeros_like(after)

    def label_message(hop):
        return pltpu.make_async_remote_copy(
            src_ref=labels.at[hop],
            dst_ref=label_in.at[me],
            send_sem=label_send.at[hop],
            recv_sem=label_recv.at[hop],
            device_id={"tile": receiver(me, hop, count)},
            device_id_type=MESH,
        )

    def message(part, hop):
        return pltpu.make_async_remote_copy(
            src_ref=outgoing.at[part, hop],
            dst_ref=arrived[part].at[pl.ds(me * capacity, capacity)],
            send_sem=send_sem.at[part, hop],
            recv_sem=recv_sem.at[part, hop],
            device_id={"tile": receiver(me, hop, count)},
            device_id_type=MESH,
        )

    def each_hop(begin, end, act):
        def one(hop, carry):
            act(hop)
            return carry

        lax.fori_loop(begin, end, one, 0)

    def piece(hop, r, part):
        return warped[route_smem[1, hop * capacity + r], part * high : (part + 1) * high, :]

    def send(part, hop):
        for r in range(capacity):
            outgoing[part, hop, r] = piece(hop, r, part)
        message(part, hop).start()

    ready = GROUP // capacity
    steps = blocks // GROUP
    each_hop(0, count - 1, lambda hop: label_message(hop).start())
    warped[...] = jnp.zeros_like(warped)
    view = lambda ref, place: ref.at[pl.ds(place[0], place[1]), pl.ds(0, place[2])]
    rows_in, rows_out, cols_in, cols_out = (view(tables, place) for place in places[:4])
    row_taps, col_taps = (view(wave_table, place) for place in places[4:])
    loads[0].wait()
    tables[...] = wave_table[: tables.shape[0], :].astype(tables.dtype)
    row_wave[...] = lax.dot_general(
        row_taps[...],
        row_bases[...].astype(jnp.float32),
        (((1,), (1,)), ((), ())),
        precision=lax.Precision.HIGHEST,
        preferred_element_type=jnp.float32,
    )
    col_wave[...] = jnp.dot(
        col_bases[...].astype(jnp.float32),
        col_taps[...],
        precision=lax.Precision.HIGHEST,
        preferred_element_type=jnp.float32,
    ).astype(col_wave.dtype)
    for load in loads[1:]:
        load.wait()
    move.wait()

    @pl.when(me > 0)
    def _():
        down.wait_recv()

    @pl.when(me < count - 1)
    def _():
        up.wait_recv()

    transform_rows(reach, rows_in, before, exposure, after, strip)

    def group(step, carry):
        match_group(
            step, route_smem, rows_out, cols_in, cols_out, row_wave, col_wave, coef_ref,
            strip, rows_ref, cols_ref, spectrum, response, warps, waves, warped,
        )
        for hop in range(ready):
            for part in range(parts):
                send(part, step * ready + hop)
        return carry

    lax.fori_loop(0, steps, group, 0)
    for part in range(parts):
        each_hop(steps * ready, count - 1, lambda hop, part=part: send(part, hop))
        for r in range(capacity):
            arrived[part][me * capacity + r] = piece(count - 1, r, part)

    label_in[me] = labels[count - 1]
    each_hop(0, count - 1, lambda hop: label_message(hop).wait())
    slot_order(label_in, table_int, table_float, weight_sum, tiles * across * across)
    moves = [
        pltpu.make_async_copy(table_int, int_smem, table_sem.at[1]),
        pltpu.make_async_copy(table_float, float_smem, table_sem.at[2]),
    ]
    for move in moves:
        move.start()

    def to_peer(hop, from_ref, to_ref, send_sem, recv_sem):
        return pltpu.make_async_remote_copy(
            src_ref=from_ref,
            dst_ref=to_ref,
            send_sem=send_sem,
            recv_sem=recv_sem,
            device_id={"src": lax.rem(my_src + hop, peers)},
            device_id_type=MESH,
        )

    def weight_message(hop):
        return to_peer(
            hop, weight_sum, weight_in.at[hop - 1], weight_send.at[hop - 1], weight_recv.at[hop - 1]
        )

    def sum_message(part, hop):
        return to_peer(
            hop,
            partial[part].at[lax.rem(my_src + hop, peers)],
            gathered[part].at[hop - 1],
            sum_send.at[part, hop - 1],
            sum_recv.at[part, hop - 1],
        )

    for hop in range(1, peers):
        weight_message(hop).start()
    for move in moves:
        move.wait()

    def stack(part):
        def add(place, total):
            block = arrived[part][int_smem[0, place]].astype(jnp.float32)
            total = total * float_smem[1, place] + float_smem[0, place] * block
            running[place] = total
            return total

        lax.fori_loop(
            0, arrived[part].shape[0], add, jnp.zeros((high, side), jnp.float32), unroll=4
        )

        def take(slot, carry):
            row = lax.rem(slot // across, across)
            place = slot // (across * across) * across + lax.rem(slot, across)
            total = running[int_smem[1, slot]] * float_smem[2, slot]
            partial[part][row, place] = total.astype(jnp.bfloat16)
            return carry

        lax.fori_loop(0, tiles * across * across, take, 0, unroll=4)

    def finish(part):
        for hop in range(1, peers):
            sum_message(part, hop).wait()
        for tile in range(tiles):
            for column in range(across):
                place = tile * across + column
                total = partial[part][my_src, place].astype(jnp.float32)
                for hop in range(peers - 1):
                    total = total + gathered[part][hop, place].astype(jnp.float32)
                slot = (tile * across + my_src) * across + column
                coadd[
                    tile, part * high : (part + 1) * high, column * side : (column + 1) * side
                ] = total * scale[slot]

    for part in range(parts):
        each_hop(0, count - 1, lambda hop, part=part: message(part, hop).wait_recv())
        stack(part)
        for hop in range(1, peers):
            sum_message(part, hop).start()
        if part == 0:
            for hop in range(1, peers):
                weight_message(hop).wait()
            weight = weight_sum[...]
            for hop in range(peers - 1):
                weight = weight + weight_in[hop]
            factor = 1.0 / jnp.maximum(weight, 1.0)
            for slot in range(scale.shape[0]):
                scale[slot] = factor[slot : slot + 1]
        else:
            finish(part - 1)
    finish(parts - 1)
    for part in range(parts):
        each_hop(0, count - 1, lambda hop, part=part: message(part, hop).wait_send())

    @pl.when(me < count - 1)
    def _():
        down.wait_send()

    @pl.when(me > 0)
    def _():
        up.wait_send()


def body(
    exposure,
    row_bases,
    col_bases,
    coefficients,
    warp_rows,
    warp_cols,
    variance,
    footprint,
    slot_index,
):
    blocks, side = warp_rows.shape[2:4]
    columns = exposure.shape[2]
    basis_count, taps = row_bases.shape
    peers, count = lax.axis_size("src"), lax.axis_size("tile")
    capacity = max(2, 2 * blocks // count)
    slots, sends = TILES_DEV * peers * peers, count * capacity
    reach = taps // 2
    tall = -(-(side + taps - 1) // 16) * 16
    tables, places = wave_tables(
        taps, side, tall, side + taps - 1, side + 2 * HALO, HALO - reach
    )
    spectra = places[0][1]
    near, far = pl.BlockSpec(memory_space=pltpu.VMEM), pl.BlockSpec(memory_space=pl.ANY)
    high, per = side // PARTS, slots // peers
    narrow, wide, whole = jnp.bfloat16, jnp.float32, jnp.int32
    vmem, smem, dma = pltpu.VMEM, pltpu.SMEM, pltpu.SemaphoreType.DMA
    return pl.pallas_call(
        functools.partial(coadd_kernel, reach, capacity, places),
        in_specs=[far] * 4 + [near] * 6,
        out_specs=near,
        out_shape=jax.ShapeDtypeStruct((TILES_DEV, side, peers * side), wide),
        scratch_shapes=[
            vmem((side, columns), narrow),
            vmem((HALO, columns), narrow),
            vmem((HALO, columns), narrow),
            vmem((columns // SPAN + 1, spectra, SPAN), narrow),
            vmem((places[4][0], 2 * SPAN), narrow),
            vmem(tables.shape, wide),
            vmem((spectra, basis_count), wide),
            vmem((basis_count, 2 * SPAN), narrow),
            vmem((blocks, 1, basis_count), wide),
            vmem((8, sends), whole),
            vmem((8, sends), whole),
            vmem((count, 8, sends), whole),
            vmem((GROUP * spectra, 2 * SPAN), wide),
            vmem((GROUP * spectra, 2 * SPAN), wide),
            vmem((GROUP * side, spectra), narrow),
            vmem((GROUP * side, 2 * SPAN), narrow),
            vmem((blocks, side, side), narrow),
            vmem((blocks, side, side), narrow),
            vmem((blocks, side, side), narrow),
            vmem((PARTS, count, capacity, high, side), narrow),
            vmem((count, 8, sends), whole),
            vmem((8, sends), whole),
            vmem((8, sends), wide),
            vmem((slots, sends), wide),
            vmem((peers - 1, slots, sends), wide),
            vmem((slots, 1, sends), wide),
            vmem((sends, high, side), wide),
            smem((8, sends), whole),
            smem((8, sends), whole),
            smem((8, sends), wide),
            dma((2,)),
            dma((2,)),
            dma((PARTS, count)),
            dma((PARTS, count)),
            dma((count,)),
            dma((count,)),
            dma((4,)),
            dma((3,)),
            dma((PARTS, peers - 1)),
            dma((PARTS, peers - 1)),
            dma((peers - 1,)),
            dma((peers - 1,)),
            *[vmem((sends, high, side), narrow) for _ in range(PARTS)],
            *[vmem((peers, per, high, side), narrow) for _ in range(PARTS)],
            *[vmem((peers - 1, per, high, side), narrow) for _ in range(PARTS)],
        ],
        compiler_params=pltpu.CompilerParams(
            collective_id=0, has_side_effects=True, vmem_limit_bytes=60 * 1024 * 1024
        ),
        cost_estimate=pl.CostEstimate(flops=4 << 30, bytes_accessed=10 << 20, transcendentals=0),
    )(
        exposure[0], warp_rows[0, 0], warp_cols[0, 0], tables, row_bases, col_bases,
        coefficients[0].transpose(2, 0, 1), variance[0], footprint.reshape(1, blocks), slot_index[0],
    )


def solution(mesh):
    placed = (
        P("src", "tile", None),
        P(),
        P(),
        P("src", "tile", None, None),
        P("src", "tile", None, None, None),
        P("src", "tile", None, None, None),
        P("src", "tile", None),
        P("src", "tile", None, None),
        P("src", "tile", None),
    )
    return jax.shard_map(
        body, mesh=mesh, in_specs=placed, out_specs=P("tile", "src", None), check_vma=False
    )
```

time: 104 us -> 102 us (0.981)
  Pallas kernels: 88.9 us -> 99.3 us
  starting transfers between devices: 5.6 us -> 0 us
  waiting for transfers between devices: 4.3 us -> 0 us
    pallas_call x1, Pallas kernels: 88.9 us -> 99.3 us  [body(): pl.pallas_call(functools.partial(coadd_kernel, reach, capacity, places),...]
    ppermute x2 -> x0, starting transfers between devices: 5.6 us -> none  [the longest x1 3.02 us: halo_rows(): before = lax.ppermute(exposure[length - width:], 'tile', up)]
    ppermute x2 -> x0, waiting for transfers between devices: 4.3 us -> none  [the longest x1 3.41 us: halo_rows(): after = lax.ppermute(exposure[:width], 'tile', down)]
    slice x1 -> x0, local copies, waits for them, and re-layouts: 1.47 us -> none  [halo_rows(): after = lax.ppermute(exposure[:width], 'tile', down)]
    unnamed x26 -> x1, local copies, waits for them, and re-layouts: 1.12 us -> 2.26 us
  transfers between devices with their start and end apart: 2 -> 0, of which waited for: 2 -> 0; matrix products, arithmetic and copies ran while one was open for 2% -> 0% of each run, Pallas kernels for 0% -> 0%
where the time goes in v2:
time: 102 us
  Pallas kernels  99.3 us (97%)
  local copies, waits for them, and re-layouts  2.26 us (2%)
    pallas_call x1, Pallas kernels, body(): pl.pallas_call(functools.partial(coadd_kernel, reach, capacity, places),...  99.3 us
    unnamed x1, local copies, waits for them, and re-layouts  2.26 us

profile of v2, /device:TPU:3, one launch (start us, length us, event | category | flops | bytes accessed | tf_op | source)
XLA Modules:
  0.0 101.6 jit_solution(13527260338132656769)
XLA Ops:
  0.0 99.3 %shard_map.100 = f32[4,128,512]{2,1,0:T(8,128)} custom-call(bf16[128,8192]{1,0:T(8,128)(2,1)} %bitcast.9, bf16[64,128,128]{2,1,0:T(8,128)(2,1)} %bitcast.10, bf16[64,128,128]{2,1,0:T(8,128)(2,1)} %bitcast.11, f32[1072,256]{1,0:T(8,128)} %constant.2.clone.tables_hbm, bf16[27,41]{1,0:T(8,128)(2,1)} %row_bases.1, bf16[27,41]{1,0:T(8,128)(2,1)} %col_bases.1, ...), custom_call_target="tpu_custom_call" | custom-call | flops 4294967296 | bytes 10485760 | tf_op jit(solution)/shard_map/pallas_call | solution.py:512
  99.3 2.3 %copy.12 = f32[4,128,512]{2,1,0:T(8,128)} copy(f32[4,128,512]{2,1,0:T(8,128)} %shard_map.100) | data formatting | bytes 2097152

commit v3 on v2

--- a/solution.py
+++ b/solution.py
@@ -12,7 +12,7 @@
 
 
 HALO = 32
-GROUP = 8
+GROUP = 4
 SPAN = 128
 
 
@@ -46,7 +46,7 @@
 
 MESH = pl.DeviceIdType.MESH
 LINE, CORES = 4, 2
-PARTS = 4
+PARTS = (32, 32, 32, 16, 16)
 WEIGHT_UNIT = 512.0
 
 
@@ -224,17 +224,19 @@
     exposure, before, after, strip, tables, wave_table, row_wave, col_wave, coef_ref,
     route_table, fields, labels,
     spectrum, response, warps, waves, warped, rows_ref, cols_ref,
-    outgoing, label_in, table_int, table_float, weight_sum, weight_in, scale, running,
+    label_in, table_int, table_float, weight_sum, weight_in, scale, running,
     route_smem, int_smem, float_smem,
     halo_send, halo_recv, send_sem, recv_sem, label_send, label_recv, load_sem, table_sem,
     sum_send, sum_recv, weight_send, weight_recv, *pieces,
 ):
-    parts = len(pieces) // 3
-    arrived, partial, gathered = pieces[:parts], pieces[parts : 2 * parts], pieces[2 * parts :]
+    parts = len(PARTS)
+    outgoing, arrived, partial, gathered = (
+        pieces[kind * parts : (kind + 1) * parts] for kind in range(4)
+    )
     me, my_src = lax.axis_index("tile"), lax.axis_index("src")
     blocks, side = warped.shape[:2]
-    count, peers = outgoing.shape[1], partial[0].shape[0]
-    high = side // parts
+    count, peers = labels.shape[0], partial[0].shape[0]
+    rows_of = [slice(sum(PARTS[:part]), sum(PARTS[: part + 1])) for part in range(parts)]
     tiles, across = coadd.shape[0], peers
     barrier, greetings = greet((("tile", count, me), ("src", peers, my_src)))
     loads = [
@@ -305,7 +307,7 @@
 
     def message(part, hop):
         return pltpu.make_async_remote_copy(
-            src_ref=outgoing.at[part, hop],
+            src_ref=outgoing[part].at[hop],
             dst_ref=arrived[part].at[pl.ds(me * capacity, capacity)],
             send_sem=send_sem.at[part, hop],
             recv_sem=recv_sem.at[part, hop],
@@ -321,11 +323,11 @@
         lax.fori_loop(begin, end, one, 0)
 
     def piece(hop, r, part):
-        return warped[route_smem[1, hop * capacity + r], part * high : (part + 1) * high, :]
+        return warped[route_smem[1, hop * capacity + r], rows_of[part], :]
 
     def send(part, hop):
         for r in range(capacity):
-            outgoing[part, hop, r] = piece(hop, r, part)
+            outgoing[part][hop, r] = piece(hop, r, part)
         message(part, hop).start()
 
     ready = GROUP // capacity
@@ -420,10 +422,12 @@
         move.wait()
 
     def stack(part):
+        high = PARTS[part]
+
         def add(place, total):
             block = arrived[part][int_smem[0, place]].astype(jnp.float32)
             total = total * float_smem[1, place] + float_smem[0, place] * block
-            running[place] = total
+            running[place, :high] = total
             return total
 
         lax.fori_loop(
@@ -433,7 +437,7 @@
         def take(slot, carry):
             row = lax.rem(slot // across, across)
             place = slot // (across * across) * across + lax.rem(slot, across)
-            total = running[int_smem[1, slot]] * float_smem[2, slot]
+            total = running[int_smem[1, slot], :high] * float_smem[2, slot]
             partial[part][row, place] = total.astype(jnp.bfloat16)
             return carry
 
@@ -449,9 +453,7 @@
                 for hop in range(peers - 1):
                     total = total + gathered[part][hop, place].astype(jnp.float32)
                 slot = (tile * across + my_src) * across + column
-                coadd[
-                    tile, part * high : (part + 1) * high, column * side : (column + 1) * side
-                ] = total * scale[slot]
+                coadd[tile, rows_of[part], column * side : (column + 1) * side] = total * scale[slot]
 
     for part in range(parts):
         each_hop(0, count - 1, lambda hop, part=part: message(part, hop).wait_recv())
@@ -505,8 +507,8 @@
         taps, side, tall, side + taps - 1, side + 2 * HALO, HALO - reach
     )
     spectra = places[0][1]
-    near, far = pl.BlockSpec(memory_space=pltpu.VMEM), pl.BlockSpec(memory_space=pl.ANY)
-    high, per = side // PARTS, slots // peers
+    near, far = pl.BlockSpec(memory_space=pltpu.VMEM), pl.BlockSpec(memory_space=pltpu.HBM)
+    parts, per = len(PARTS), slots // peers
     narrow, wide, whole = jnp.bfloat16, jnp.float32, jnp.int32
     vmem, smem, dma = pltpu.VMEM, pltpu.SMEM, pltpu.SemaphoreType.DMA
     return pl.pallas_call(
@@ -534,35 +536,35 @@
             vmem((blocks, side, side), narrow),
             vmem((blocks, side, side), narrow),
             vmem((blocks, side, side), narrow),
-            vmem((PARTS, count, capacity, high, side), narrow),
             vmem((count, 8, sends), whole),
             vmem((8, sends), whole),
             vmem((8, sends), wide),
             vmem((slots, sends), wide),
             vmem((peers - 1, slots, sends), wide),
             vmem((slots, 1, sends), wide),
-            vmem((sends, high, side), wide),
+            vmem((sends, max(PARTS), side), wide),
             smem((8, sends), whole),
             smem((8, sends), whole),
             smem((8, sends), wide),
             dma((2,)),
             dma((2,)),
-            dma((PARTS, count)),
-            dma((PARTS, count)),
+            dma((parts, count)),
+            dma((parts, count)),
             dma((count,)),
             dma((count,)),
             dma((4,)),
             dma((3,)),
-            dma((PARTS, peers - 1)),
-            dma((PARTS, peers - 1)),
+            dma((parts, peers - 1)),
+            dma((parts, peers - 1)),
             dma((peers - 1,)),
             dma((peers - 1,)),
-            *[vmem((sends, high, side), narrow) for _ in range(PARTS)],
-            *[vmem((peers, per, high, side), narrow) for _ in range(PARTS)],
-            *[vmem((peers - 1, per, high, side), narrow) for _ in range(PARTS)],
+            *[vmem((count, capacity, high, side), narrow) for high in PARTS],
+            *[vmem((sends, high, side), narrow) for high in PARTS],
+            *[vmem((peers, per, high, side), narrow) for high in PARTS],
+            *[vmem((peers - 1, per, high, side), narrow) for high in PARTS],
         ],
         compiler_params=pltpu.CompilerParams(
-            collective_id=0, has_side_effects=True, vmem_limit_bytes=60 * 1024 * 1024
+            collective_id=0, has_side_effects=True, vmem_limit_bytes=50 * 1024 * 1024
         ),
         cost_estimate=pl.CostEstimate(flops=4 << 30, bytes_accessed=10 << 20, transcendentals=0),
     )(

time: 102 us -> 107 us (1.049)
  local copies, waits for them, and re-layouts: 2.26 us -> 6.28 us
    unnamed x1 -> x15, local copies, waits for them, and re-layouts: 2.26 us -> 6.28 us
    pallas_call x1, Pallas kernels: 99.3 us -> 100 us  [body(): pl.pallas_call(functools.partial(coadd_kernel, reach, capacity, places),...]
where the time goes in v3:
time: 107 us
  Pallas kernels  100 us (93%)
  local copies, waits for them, and re-layouts  6.28 us (6%)
    pallas_call x1, Pallas kernels, body(): pl.pallas_call(functools.partial(coadd_kernel, reach, capacity, places),...  100 us
    unnamed x15, local copies, waits for them, and re-layouts  6.28 us

profile of v3, /device:TPU:3, one launch (start us, length us, event | category | flops | bytes accessed | tf_op | source)
XLA Modules:
  0.0 106.8 jit_solution(8809677079996352293)
XLA Ops:
  0.0 0.0 copy-start
  0.0 0.7 copy-done
  0.7 0.0 copy-start.1
  0.7 0.7 copy-done.1
  1.4 0.0 copy-start.2
  1.4 0.7 copy-done.2
  2.1 0.0 copy-start.3
  2.1 0.7 copy-done.3
  2.8 0.0 copy-start.4
  2.8 0.7 copy-done.4
  3.4 0.0 copy-start.5
  3.4 0.7 copy-done.5
  4.1 0.0 copy-start.6
  4.1 1.2 %copy-done.6 = f32[1072,256]{1,0:T(8,128)S(1)} copy-done((f32[1072,256]{1,0:T(8,128)S(1)}, f32[1072,256]{1,0:T(8,128)}, u32[]{:S(2)}) %copy-start.6) | copy-done | bytes 1097752
  5.3 100.5 %shard_map.100 = f32[4,128,512]{2,1,0:T(8,128)S(1)} custom-call(bf16[128,8192]{1,0:T(8,128)(2,1)} %bitcast.13, bf16[64,128,128]{2,1,0:T(8,128)(2,1)} %bitcast.14, bf16[64,128,128]{2,1,0:T(8,128)(2,1)} %bitcast.15, f32[1072,256]{1,0:T(8,128)S(1)} %copy-done.6, bf16[27,41]{1,0:T(8,128)(2,1)S(1)} %copy-done.1, bf16[27,41]{1,0:T(8,128)(2,1)S(1)} %copy-done.2, ...), custom_call_target="tpu_custom_call" | custom-call | flops 4294967296 | bytes 10485760 | tf_op jit(solution)/shard_map/pallas_call | solution.py:514
  105.8 1.0 copy.12
Async XLA Ops:
  0.0 0.7 copy-start
  0.7 0.7 copy-start.1
  1.4 0.7 copy-start.2
  2.1 0.7 copy-start.3
  2.8 0.7 copy-start.4
  3.4 0.7 copy-start.5
  4.1 1.2 %copy-start.6 = (f32[1072,256]{1,0:T(8,128)S(1)}, f32[1072,256]{1,0:T(8,128)}, u32[]{:S(2)}) copy-start(f32[1072,256]{1,0:T(8,128)} %constant.2.clone.tables_hbm) | copy-start | bytes 3293188

commit v4 on v3

--- a/solution.py
+++ b/solution.py
@@ -11,22 +11,24 @@
 TILES_DEV = 4
 
 
-HALO = 32
+EDGE = 16
+FOLDS = 4
 GROUP = 4
 SPAN = 128
 
 
-def wave_tables(taps, side, tall, wide, frame, skip):
+def wave_tables(taps, side, tall, wide):
     low, lanes = -(-(tall // 2 + 1) // 16) * 16, SPAN
     u, v = np.arange(low), np.arange(lanes)
     keep_u, keep_v = u <= tall // 2, v <= wide // 2
     twice_u = np.where((u == 0) | (2 * u == tall), 1.0, 2.0) * keep_u
     twice_v = np.where((v == 0) | (2 * v == wide), 1.0, 2.0) * keep_v
     turn = lambda one, other, length: 2.0 * np.pi / length * (np.outer(one, other) % length)
-    place = np.arange(frame) - skip
-    down = turn(u, place, tall)
-    used = (place >= 0) & (place < side + taps - 1)
-    rows_in = np.concatenate([np.cos(down), np.sin(down)]) * np.tile(keep_u, 2)[:, None] * used
+    reach, edge = taps // 2, np.arange(EDGE)
+    fold = edge % (reach - EDGE)
+    starts = (reach + np.arange(side), reach - EDGE + edge, reach + side + edge, fold, reach + side + EDGE + fold)
+    down = turn(u, np.concatenate(starts), tall)
+    rows_in = np.concatenate([np.cos(down), np.sin(down)]) * np.tile(keep_u, 2)[:, None]
     back = turn(np.arange(side), u, tall)
     rows_out = np.concatenate([np.cos(back) * twice_u, -np.sin(back) * twice_u], axis=1) / tall
     along = turn(np.arange(2 * side), v, wide)
@@ -106,15 +108,31 @@
     fields[...] = jnp.concatenate(row + [jnp.zeros_like(row[0])] * (fields.shape[0] - 2), axis=0)
 
 
-def transform_rows(reach, rows_in, before, exposure, after, strip):
+def fold_rows(rows):
+    part = rows.shape[1] // FOLDS
+    zeros = jnp.zeros((rows.shape[0], SPAN), rows.dtype)
+    quarters = []
+    for fold in range(FOLDS):
+        begin = fold * part
+        ahead = rows[:, begin - SPAN : begin] if fold else zeros
+        quarters.append(jnp.concatenate([ahead, rows[:, begin : begin + part]], axis=1))
+    return jnp.concatenate(quarters, axis=0)
+
+
+def transform_rows(reach, rows_in, exposure, edges, folds, strip):
     columns = exposure.shape[1]
     tiles = 4
     wide = tiles * SPAN
+    per_fold = columns // wide // FOLDS
+    fold_of_row = lax.broadcasted_iota(jnp.int32, (EDGE, 1), 0) // (EDGE // FOLDS)
 
     def rows(begin, width):
-        return jnp.concatenate(
-            [ref[:, pl.ds(begin, width)] for ref in (before, exposure, after)], axis=0
-        )
+        return jnp.concatenate([ref[:, pl.ds(begin, width)] for ref in (exposure, *edges)], axis=0)
+
+    def folded(fold, begin, width):
+        pieces = [ref[:, pl.ds(begin, width)] for ref in folds]
+        mine = fold_of_row == fold
+        return jnp.concatenate([jnp.where(mine, piece, 0) for piece in pieces], axis=0)
 
     def spectra(window):
         return jnp.dot(rows_in[...], window, preferred_element_type=jnp.float32).astype(strip.dtype)
@@ -125,14 +143,22 @@
             strip[number * tiles + tile] = moved[:, tile * SPAN : (tile + 1) * SPAN]
 
     def piece(number, carry):
-        begin = pl.multiple_of(number * wide, wide)
-        store(number, rows(pl.multiple_of(begin - SPAN, SPAN), wide + SPAN))
+        begin = pl.multiple_of(number * wide - SPAN, SPAN)
+        inside = pl.multiple_of(lax.rem(number, per_fold) * wide, wide)
+        over = wide + SPAN
+        store(
+            number,
+            jnp.concatenate([rows(begin, over), folded(number // per_fold, inside, over)], axis=0),
+        )
         return carry
 
-    zeros = jnp.zeros((rows_in.shape[1], SPAN), exposure.dtype)
-    store(0, jnp.concatenate([zeros, rows(0, wide)], axis=1))
+    total = exposure.shape[0] + EDGE * (len(edges) + len(folds))
+    zeros = jnp.zeros((total, SPAN), exposure.dtype)
+    first = jnp.concatenate([rows(0, wide), folded(0, SPAN, wide)], axis=0)
+    store(0, jnp.concatenate([zeros, first], axis=1))
     lax.fori_loop(1, columns // wide, piece, 0)
-    last = jnp.concatenate([rows(columns - SPAN, SPAN), zeros], axis=1)
+    last = [rows(columns - SPAN, SPAN), folded(FOLDS - 1, columns // FOLDS, SPAN)]
+    last = jnp.concatenate([jnp.concatenate(last, axis=0), zeros], axis=1)
     strip[columns // SPAN] = spectra(last[:, SPAN - reach : 2 * SPAN - reach])
 
 
@@ -221,7 +247,7 @@
 def coadd_kernel(
     reach, capacity, places, exposure_hbm, rows_hbm, cols_hbm, tables_hbm,
     row_bases, col_bases, coefficients, variance, owner, slot_index, coadd,
-    exposure, before, after, strip, tables, wave_table, row_wave, col_wave, coef_ref,
+    exposure, before, after, fold_before, fold_after, fold_down, fold_up, strip, tables, wave_table, row_wave, col_wave, coef_ref,
     route_table, fields, labels,
     spectrum, response, warps, waves, warped, rows_ref, cols_ref,
     label_in, table_int, table_float, weight_sum, weight_in, scale, running,
@@ -264,11 +290,15 @@
             fields[...], lax.rem((me - hop + count) * capacity, lane.shape[1]), axis=1
         )
         labels[hop] = jnp.where(lane // capacity == me, moved, 0)
+    loads[1].wait()
+    spare = reach - EDGE
+    fold_down[...] = fold_rows(exposure[side - 2 * EDGE : side - EDGE, :][EDGE - spare :, :])
+    fold_up[...] = fold_rows(exposure[EDGE : 2 * EDGE, :][:spare, :])
     pl.semaphore_wait(barrier, greetings)
 
-    def halo(number, begin, to_ref, neighbour):
+    def halo(number, from_ref, to_ref, neighbour):
         return pltpu.make_async_remote_copy(
-            src_ref=exposure_hbm.at[pl.ds(begin, HALO)],
+            src_ref=from_ref,
             dst_ref=to_ref,
             send_sem=halo_send.at[number],
             recv_sem=halo_recv.at[number],
@@ -276,24 +306,32 @@
             device_id_type=MESH,
         )
 
-    down = halo(0, side - HALO, before, lax.rem(me + 1, count))
-    up = halo(1, 0, after, lax.rem(me + count - 1, count))
+    below, above = lax.rem(me + 1, count), lax.rem(me + count - 1, count)
+    down = (
+        halo(0, exposure.at[pl.ds(side - EDGE, EDGE)], before, below),
+        halo(1, fold_down, fold_before, below),
+    )
+    up = (halo(2, exposure.at[pl.ds(0, EDGE)], after, above), halo(3, fold_up, fold_after, above))
 
     @pl.when(me < count - 1)
     def _():
-        down.start()
+        for copy in down:
+            copy.start()
 
     @pl.when(me > 0)
     def _():
-        up.start()
+        for copy in up:
+            copy.start()
 
     @pl.when(me == 0)
     def _():
         before[...] = jnp.zeros_like(before)
+        fold_before[...] = jnp.zeros_like(fold_before)
 
     @pl.when(me == count - 1)
     def _():
         after[...] = jnp.zeros_like(after)
+        fold_after[...] = jnp.zeros_like(fold_after)
 
     def label_message(hop):
         return pltpu.make_async_remote_copy(
@@ -352,19 +390,21 @@
         precision=lax.Precision.HIGHEST,
         preferred_element_type=jnp.float32,
     ).astype(col_wave.dtype)
-    for load in loads[1:]:
+    for load in loads[2:]:
         load.wait()
     move.wait()
 
     @pl.when(me > 0)
     def _():
-        down.wait_recv()
+        for copy in down:
+            copy.wait_recv()
 
     @pl.when(me < count - 1)
     def _():
-        up.wait_recv()
-
-    transform_rows(reach, rows_in, before, exposure, after, strip)
+        for copy in up:
+            copy.wait_recv()
+
+    transform_rows(reach, rows_in, exposure, (before, after), (fold_before, fold_after), strip)
 
     def group(step, carry):
         match_group(
@@ -477,11 +517,13 @@
 
     @pl.when(me < count - 1)
     def _():
-        down.wait_send()
+        for copy in down:
+            copy.wait_send()
 
     @pl.when(me > 0)
     def _():
-        up.wait_send()
+        for copy in up:
+            copy.wait_send()
 
 
 def body(
@@ -504,10 +546,10 @@
     reach = taps // 2
     tall = -(-(side + taps - 1) // 16) * 16
     tables, places = wave_tables(
-        taps, side, tall, side + taps - 1, side + 2 * HALO, HALO - reach
+        taps, side, tall, side + taps - 1
     )
     spectra = places[0][1]
-    near, far = pl.BlockSpec(memory_space=pltpu.VMEM), pl.BlockSpec(memory_space=pltpu.HBM)
+    near, far = pl.BlockSpec(memory_space=pltpu.VMEM), pl.BlockSpec(memory_space=pl.ANY)
     parts, per = len(PARTS), slots // peers
     narrow, wide, whole = jnp.bfloat16, jnp.float32, jnp.int32
     vmem, smem, dma = pltpu.VMEM, pltpu.SMEM, pltpu.SemaphoreType.DMA
@@ -518,8 +560,9 @@
         out_shape=jax.ShapeDtypeStruct((TILES_DEV, side, peers * side), wide),
         scratch_shapes=[
             vmem((side, columns), narrow),
-            vmem((HALO, columns), narrow),
-            vmem((HALO, columns), narrow),
+            vmem((EDGE, columns), narrow),
+            vmem((EDGE, columns), narrow),
+            *[vmem((EDGE, columns // FOLDS + SPAN), narrow)] * 4,
             vmem((columns // SPAN + 1, spectra, SPAN), narrow),
             vmem((places[4][0], 2 * SPAN), narrow),
             vmem(tables.shape, wide),
@@ -546,8 +589,8 @@
             smem((8, sends), whole),
             smem((8, sends), whole),
             smem((8, sends), wide),
-            dma((2,)),
-            dma((2,)),
+            dma((4,)),
+            dma((4,)),
             dma((parts, count)),
             dma((parts, count)),
             dma((count,)),
@@ -564,7 +607,7 @@
             *[vmem((peers - 1, per, high, side), narrow) for high in PARTS],
         ],
         compiler_params=pltpu.CompilerParams(
-            collective_id=0, has_side_effects=True, vmem_limit_bytes=50 * 1024 * 1024
+            collective_id=0, has_side_effects=True, vmem_limit_bytes=60 * 1024 * 1024
         ),
         cost_estimate=pl.CostEstimate(flops=4 << 30, bytes_accessed=10 << 20, transcendentals=0),
     )(

time: 107 us -> 102 us (0.953)
  local copies, waits for them, and re-layouts: 6.28 us -> 2.26 us
    unnamed x15 -> x1, local copies, waits for them, and re-layouts: 6.28 us -> 2.26 us
    pallas_call x1, Pallas kernels: 100 us -> 99.4 us  [body(): pl.pallas_call(functools.partial(coadd_kernel, reach, capacity, places),...]
where the time goes in v4:
time: 102 us
  Pallas kernels  99.4 us (97%)
  local copies, waits for them, and re-layouts  2.26 us (2%)
    pallas_call x1, Pallas kernels, body(): pl.pallas_call(functools.partial(coadd_kernel, reach, capacity, places),...  99.4 us
    unnamed x1, local copies, waits for them, and re-layouts  2.26 us

profile of v4, /device:TPU:3, one launch (start us, length us, event | category | flops | bytes accessed | tf_op | source)
XLA Modules:
  0.0 101.7 jit_solution(2824849036994716233)
XLA Ops:
  0.0 99.4 %shard_map.100 = f32[4,128,512]{2,1,0:T(8,128)} custom-call(bf16[128,8192]{1,0:T(8,128)(2,1)} %bitcast.9, bf16[64,128,128]{2,1,0:T(8,128)(2,1)} %bitcast.10, bf16[64,128,128]{2,1,0:T(8,128)(2,1)} %bitcast.11, f32[1072,256]{1,0:T(8,128)} %constant.2.clone.tables_hbm, bf16[27,41]{1,0:T(8,128)(2,1)} %row_bases.1, bf16[27,41]{1,0:T(8,128)(2,1)} %col_bases.1, ...), custom_call_target="tpu_custom_call" | custom-call | flops 4294967296 | bytes 10485760 | tf_op jit(solution)/shard_map/pallas_call | solution.py:556
  99.4 2.3 %copy.12 = f32[4,128,512]{2,1,0:T(8,128)} copy(f32[4,128,512]{2,1,0:T(8,128)} %shard_map.100) | data formatting | bytes 2097152

commit v5 on v4

--- a/solution.py
+++ b/solution.py
@@ -13,7 +13,7 @@
 
 EDGE = 16
 FOLDS = 4
-GROUP = 4
+GROUP = 8
 SPAN = 128
 
 
@@ -48,7 +48,7 @@
 
 MESH = pl.DeviceIdType.MESH
 LINE, CORES = 4, 2
-PARTS = (32, 32, 32, 16, 16)
+PARTS = (48, 32, 32, 16)
 WEIGHT_UNIT = 512.0
 
 
@@ -224,6 +224,8 @@
     down, along = (lax.broadcasted_iota(jnp.int32, square, axis) for axis in (0, 1))
     slot_along = jnp.broadcast_to(labels[1:2], square)
     weight_along = jnp.broadcast_to(labels[0:1].astype(jnp.float32) / WEIGHT_UNIT, square)
+    late = along // (places // 2) * slots
+    slot_plain, slot_along = slot_along, slot_along + late
     slot_down, weight_down = slot_along.T, weight_along.T
     ahead = (slot_along < slot_down) | ((slot_along == slot_down) & (along < down))
     rank = jnp.sum(ahead.astype(jnp.int32), axis=1, keepdims=True)
@@ -234,13 +236,14 @@
     goes_on = ((slot == pltpu.roll(slot, 1, axis=1)) & (along[:1] > 0)).astype(jnp.float32)
     up_to = jnp.sum((slot_down <= along).astype(jnp.int32), axis=0, keepdims=True)
     inside = jnp.sum((slot_down == along).astype(jnp.int32), axis=0, keepdims=True)
-    last = jnp.maximum(up_to - 1, 0)
+    half = late[:1] // slots * (places // 2)
+    order, last = order - half, jnp.maximum(up_to - 1 - half, 0)
     table_int[...] = jnp.concatenate([order, last] + [order] * (table_int.shape[0] - 2), axis=0)
     table_float[...] = jnp.concatenate(
         [weight, goes_on, (inside > 0).astype(jnp.float32)] + [weight] * (table_float.shape[0] - 3),
         axis=0,
     )
-    mine = jnp.where(slot_along[:slots] == down[:slots], weight_along[:slots], 0.0)
+    mine = jnp.where(slot_plain[:slots] == down[:slots], weight_along[:slots], 0.0)
     weight_sum[...] = jnp.broadcast_to(jnp.sum(mine, axis=1, keepdims=True), (slots, places))
 
 
@@ -250,15 +253,17 @@
     exposure, before, after, fold_before, fold_after, fold_down, fold_up, strip, tables, wave_table, row_wave, col_wave, coef_ref,
     route_table, fields, labels,
     spectrum, response, warps, waves, warped, rows_ref, cols_ref,
+    blocks_out, blocks_in, block_sums, base,
     label_in, table_int, table_float, weight_sum, weight_in, scale, running,
     route_smem, int_smem, float_smem,
-    halo_send, halo_recv, send_sem, recv_sem, label_send, label_recv, load_sem, table_sem,
+    halo_send, halo_recv, early_send, early_recv, send_sem, recv_sem, label_send, label_recv, load_sem, table_sem,
     sum_send, sum_recv, weight_send, weight_recv, *pieces,
 ):
     parts = len(PARTS)
     outgoing, arrived, partial, gathered = (
         pieces[kind * parts : (kind + 1) * parts] for kind in range(4)
     )
+    early = blocks_out.shape[0]
     me, my_src = lax.axis_index("tile"), lax.axis_index("src")
     blocks, side = warped.shape[:2]
     count, peers = labels.shape[0], partial[0].shape[0]
@@ -286,10 +291,7 @@
         coef_ref[number] = by_block[number : number + 1, :]
     lane = lax.broadcasted_iota(jnp.int32, fields.shape, 1)
     for hop in range(count):
-        moved = pltpu.roll(
-            fields[...], lax.rem((me - hop + count) * capacity, lane.shape[1]), axis=1
-        )
-        labels[hop] = jnp.where(lane // capacity == me, moved, 0)
+        labels[hop] = jnp.where(lane // capacity == hop, fields[...], 0)
     loads[1].wait()
     spare = reach - EDGE
     fold_down[...] = fold_rows(exposure[side - 2 * EDGE : side - EDGE, :][EDGE - spare :, :])
@@ -336,19 +338,29 @@
     def label_message(hop):
         return pltpu.make_async_remote_copy(
             src_ref=labels.at[hop],
-            dst_ref=label_in.at[me],
+            dst_ref=label_in.at[hop],
             send_sem=label_send.at[hop],
             recv_sem=label_recv.at[hop],
             device_id={"tile": receiver(me, hop, count)},
             device_id_type=MESH,
         )
 
+    def early_message(hop):
+        return pltpu.make_async_remote_copy(
+            src_ref=blocks_out.at[hop],
+            dst_ref=blocks_in.at[pl.ds(hop * capacity, capacity)],
+            send_sem=early_send.at[hop],
+            recv_sem=early_recv.at[hop],
+            device_id={"tile": receiver(me, hop, count)},
+            device_id_type=MESH,
+        )
+
     def message(part, hop):
         return pltpu.make_async_remote_copy(
-            src_ref=outgoing[part].at[hop],
-            dst_ref=arrived[part].at[pl.ds(me * capacity, capacity)],
-            send_sem=send_sem.at[part, hop],
-            recv_sem=recv_sem.at[part, hop],
+            src_ref=outgoing[part].at[hop - early],
+            dst_ref=arrived[part].at[pl.ds((hop - early) * capacity, capacity)],
+            send_sem=send_sem.at[part, hop - early],
+            recv_sem=recv_sem.at[part, hop - early],
             device_id={"tile": receiver(me, hop, count)},
             device_id_type=MESH,
         )
@@ -365,7 +377,7 @@
 
     def send(part, hop):
         for r in range(capacity):
-            outgoing[part][hop, r] = piece(hop, r, part)
+            outgoing[part][hop - early, r] = piece(hop, r, part)
         message(part, hop).start()
 
     ready = GROUP // capacity
@@ -411,18 +423,20 @@
             step, route_smem, rows_out, cols_in, cols_out, row_wave, col_wave, coef_ref,
             strip, rows_ref, cols_ref, spectrum, response, warps, waves, warped,
         )
-        for hop in range(ready):
-            for part in range(parts):
-                send(part, step * ready + hop)
+        for number in range(ready):
+            hop = step * ready + number
+            for r in range(capacity):
+                blocks_out[hop, r] = warped[route_smem[1, hop * capacity + r]]
+            early_message(hop).start()
         return carry
 
     lax.fori_loop(0, steps, group, 0)
     for part in range(parts):
-        each_hop(steps * ready, count - 1, lambda hop, part=part: send(part, hop))
+        each_hop(early, count - 1, lambda hop, part=part: send(part, hop))
         for r in range(capacity):
-            arrived[part][me * capacity + r] = piece(count - 1, r, part)
-
-    label_in[me] = labels[count - 1]
+            arrived[part][(count - 1 - early) * capacity + r] = piece(count - 1, r, part)
+
+    label_in[count - 1] = labels[count - 1]
     each_hop(0, count - 1, lambda hop: label_message(hop).wait())
     slot_order(label_in, table_int, table_float, weight_sum, tiles * across * across)
     moves = [
@@ -461,27 +475,43 @@
     for move in moves:
         move.wait()
 
+    half = blocks_in.shape[0]
+    slots = tiles * across * across
+
+    def stack_early():
+        def add(place, total):
+            block = blocks_in[int_smem[0, place]].astype(jnp.float32)
+            total = total * float_smem[1, place] + float_smem[0, place] * block
+            block_sums[place] = total
+            return total
+
+        lax.fori_loop(0, half, add, jnp.zeros((side, side), jnp.float32))
+
+        def take(slot, carry):
+            base[slot] = block_sums[int_smem[1, slot]] * float_smem[2, slot]
+            return carry
+
+        lax.fori_loop(0, slots, take, 0)
+
     def stack(part):
         high = PARTS[part]
 
         def add(place, total):
-            block = arrived[part][int_smem[0, place]].astype(jnp.float32)
-            total = total * float_smem[1, place] + float_smem[0, place] * block
+            block = arrived[part][int_smem[0, half + place]].astype(jnp.float32)
+            total = total * float_smem[1, half + place] + float_smem[0, half + place] * block
             running[place, :high] = total
             return total
 
-        lax.fori_loop(
-            0, arrived[part].shape[0], add, jnp.zeros((high, side), jnp.float32), unroll=4
-        )
+        lax.fori_loop(0, half, add, jnp.zeros((high, side), jnp.float32), unroll=4)
 
         def take(slot, carry):
             row = lax.rem(slot // across, across)
             place = slot // (across * across) * across + lax.rem(slot, across)
-            total = running[int_smem[1, slot], :high] * float_smem[2, slot]
-            partial[part][row, place] = total.astype(jnp.bfloat16)
+            total = running[int_smem[1, slots + slot], :high] * float_smem[2, slots + slot]
+            partial[part][row, place] = (total + base[slot, rows_of[part], :]).astype(jnp.bfloat16)
             return carry
 
-        lax.fori_loop(0, tiles * across * across, take, 0, unroll=4)
+        lax.fori_loop(0, slots, take, 0, unroll=4)
 
     def finish(part):
         for hop in range(1, peers):
@@ -495,8 +525,10 @@
                 slot = (tile * across + my_src) * across + column
                 coadd[tile, rows_of[part], column * side : (column + 1) * side] = total * scale[slot]
 
+    each_hop(0, early, lambda hop: early_message(hop).wait_recv())
+    stack_early()
     for part in range(parts):
-        each_hop(0, count - 1, lambda hop, part=part: message(part, hop).wait_recv())
+        each_hop(early, count - 1, lambda hop, part=part: message(part, hop).wait_recv())
         stack(part)
         for hop in range(1, peers):
             sum_message(part, hop).start()
@@ -513,7 +545,8 @@
             finish(part - 1)
     finish(parts - 1)
     for part in range(parts):
-        each_hop(0, count - 1, lambda hop, part=part: message(part, hop).wait_send())
+        each_hop(early, count - 1, lambda hop, part=part: message(part, hop).wait_send())
+    each_hop(0, early, lambda hop: early_message(hop).wait_send())
 
     @pl.when(me < count - 1)
     def _():
@@ -551,6 +584,8 @@
     spectra = places[0][1]
     near, far = pl.BlockSpec(memory_space=pltpu.VMEM), pl.BlockSpec(memory_space=pl.ANY)
     parts, per = len(PARTS), slots // peers
+    early = blocks // capacity
+    late = count - early
     narrow, wide, whole = jnp.bfloat16, jnp.float32, jnp.int32
     vmem, smem, dma = pltpu.VMEM, pltpu.SMEM, pltpu.SemaphoreType.DMA
     return pl.pallas_call(
@@ -579,20 +614,26 @@
             vmem((blocks, side, side), narrow),
             vmem((blocks, side, side), narrow),
             vmem((blocks, side, side), narrow),
+            vmem((early, capacity, side, side), narrow),
+            vmem((early * capacity, side, side), narrow),
+            vmem((early * capacity, side, side), wide),
+            vmem((slots, side, side), wide),
             vmem((count, 8, sends), whole),
             vmem((8, sends), whole),
             vmem((8, sends), wide),
             vmem((slots, sends), wide),
             vmem((peers - 1, slots, sends), wide),
             vmem((slots, 1, sends), wide),
-            vmem((sends, max(PARTS), side), wide),
+            vmem((late * capacity, max(PARTS), side), wide),
             smem((8, sends), whole),
             smem((8, sends), whole),
             smem((8, sends), wide),
             dma((4,)),
             dma((4,)),
-            dma((parts, count)),
-            dma((parts, count)),
+            dma((early,)),
+            dma((early,)),
+            dma((parts, late)),
+            dma((parts, late)),
             dma((count,)),
             dma((count,)),
             dma((4,)),
@@ -601,8 +642,8 @@
             dma((parts, peers - 1)),
             dma((peers - 1,)),
             dma((peers - 1,)),
-            *[vmem((count, capacity, high, side), narrow) for high in PARTS],
-            *[vmem((sends, high, side), narrow) for high in PARTS],
+            *[vmem((late, capacity, high, side), narrow) for high in PARTS],
+            *[vmem((late * capacity, high, side), narrow) for high in PARTS],
             *[vmem((peers, per, high, side), narrow) for high in PARTS],
             *[vmem((peers - 1, per, high, side), narrow) for high in PARTS],
         ],

time: 102 us -> 103 us (level)
  Pallas kernels: 99.4 us -> 101 us
    pallas_call x1, Pallas kernels: 99.4 us -> 101 us  [body(): pl.pallas_call(functools.partial(coadd_kernel, reach, capacity, places),...]
where the time goes in v5:
time: 103 us
  Pallas kernels  101 us (98%)
  local copies, waits for them, and re-layouts  2.26 us (2%)
    pallas_call x1, Pallas kernels, body(): pl.pallas_call(functools.partial(coadd_kernel, reach, capacity, places),...  101 us
    unnamed x1, local copies, waits for them, and re-layouts  2.26 us

profile of v5, /device:TPU:3, one launch (start us, length us, event | category | flops | bytes accessed | tf_op | source)
XLA Modules:
  0.0 103.0 jit_solution(7659715023794283695)
XLA Ops:
  0.0 100.8 %shard_map.100 = f32[4,128,512]{2,1,0:T(8,128)} custom-call(bf16[128,8192]{1,0:T(8,128)(2,1)} %bitcast.9, bf16[64,128,128]{2,1,0:T(8,128)(2,1)} %bitcast.10, bf16[64,128,128]{2,1,0:T(8,128)(2,1)} %bitcast.11, f32[1072,256]{1,0:T(8,128)} %constant.2.clone.tables_hbm, bf16[27,41]{1,0:T(8,128)(2,1)} %row_bases.1, bf16[27,41]{1,0:T(8,128)(2,1)} %col_bases.1, ...), custom_call_target="tpu_custom_call" | custom-call | flops 4294967296 | bytes 10485760 | tf_op jit(solution)/shard_map/pallas_call | solution.py:591
  100.8 2.3 %copy.12 = f32[4,128,512]{2,1,0:T(8,128)} copy(f32[4,128,512]{2,1,0:T(8,128)} %shard_map.100) | data formatting | bytes 2097152

commit v6 on v4

--- a/solution.py
+++ b/solution.py
@@ -13,7 +13,7 @@
 
 EDGE = 16
 FOLDS = 4
-GROUP = 4
+GROUP = 8
 SPAN = 128
 
 
@@ -48,7 +48,7 @@
 
 MESH = pl.DeviceIdType.MESH
 LINE, CORES = 4, 2
-PARTS = (32, 32, 32, 16, 16)
+PARTS = (32, 32, 32, 32)
 WEIGHT_UNIT = 512.0
 
 

time: 102 us -> 99.2 us (0.973)
  Pallas kernels: 99.4 us -> 96.7 us
    pallas_call x1, Pallas kernels: 99.4 us -> 96.7 us  [body(): pl.pallas_call(functools.partial(coadd_kernel, reach, capacity, places),...]
where the time goes in v6:
time: 99.2 us; the launch traced here: 99 us
  Pallas kernels  96.7 us (97%)
  local copies, waits for them, and re-layouts  2.26 us (2%)
    pallas_call x1, Pallas kernels, body(): pl.pallas_call(functools.partial(coadd_kernel, reach, capacity, places),...  96.7 us
    unnamed x1, local copies, waits for them, and re-layouts  2.26 us

profile of v6, /device:TPU:3, one launch (start us, length us, event | category | flops | bytes accessed | tf_op | source)
XLA Modules:
  0.0 99.0 jit_solution(6490946895962298497)
XLA Ops:
  0.0 96.7 %shard_map.100 = f32[4,128,512]{2,1,0:T(8,128)} custom-call(bf16[128,8192]{1,0:T(8,128)(2,1)} %bitcast.9, bf16[64,128,128]{2,1,0:T(8,128)(2,1)} %bitcast.10, bf16[64,128,128]{2,1,0:T(8,128)(2,1)} %bitcast.11, f32[1072,256]{1,0:T(8,128)} %constant.2.clone.tables_hbm, bf16[27,41]{1,0:T(8,128)(2,1)} %row_bases.1, bf16[27,41]{1,0:T(8,128)(2,1)} %col_bases.1, ...), custom_call_target="tpu_custom_call" | custom-call | flops 4294967296 | bytes 10485760 | tf_op jit(solution)/shard_map/pallas_call | solution.py:556
  96.8 2.3 %copy.12 = f32[4,128,512]{2,1,0:T(8,128)} copy(f32[4,128,512]{2,1,0:T(8,128)} %shard_map.100) | data formatting | bytes 2097152

commit v7 on v6

--- a/solution.py
+++ b/solution.py
@@ -119,70 +119,82 @@
     return jnp.concatenate(quarters, axis=0)
 
 
-def transform_rows(reach, rows_in, exposure, edges, folds, strip):
-    columns = exposure.shape[1]
-    tiles = 4
-    wide = tiles * SPAN
-    per_fold = columns // wide // FOLDS
-    fold_of_row = lax.broadcasted_iota(jnp.int32, (EDGE, 1), 0) // (EDGE // FOLDS)
-
-    def rows(begin, width):
-        return jnp.concatenate([ref[:, pl.ds(begin, width)] for ref in (exposure, *edges)], axis=0)
-
-    def folded(fold, begin, width):
-        pieces = [ref[:, pl.ds(begin, width)] for ref in folds]
-        mine = fold_of_row == fold
-        return jnp.concatenate([jnp.where(mine, piece, 0) for piece in pieces], axis=0)
-
-    def spectra(window):
-        return jnp.dot(rows_in[...], window, preferred_element_type=jnp.float32).astype(strip.dtype)
+def each_window(reach, columns, rows, use):
+    wide = 4 * SPAN
 
     def store(number, old):
-        moved = spectra(old[:, SPAN - reach : SPAN - reach + wide])
-        for tile in range(tiles):
-            strip[number * tiles + tile] = moved[:, tile * SPAN : (tile + 1) * SPAN]
+        use(number * 4, old[:, SPAN - reach : SPAN - reach + wide])
 
     def piece(number, carry):
-        begin = pl.multiple_of(number * wide - SPAN, SPAN)
-        inside = pl.multiple_of(lax.rem(number, per_fold) * wide, wide)
-        over = wide + SPAN
-        store(
-            number,
-            jnp.concatenate([rows(begin, over), folded(number // per_fold, inside, over)], axis=0),
-        )
+        store(number, rows(number, pl.multiple_of(number * wide - SPAN, SPAN), wide + SPAN))
         return carry
 
-    total = exposure.shape[0] + EDGE * (len(edges) + len(folds))
-    zeros = jnp.zeros((total, SPAN), exposure.dtype)
-    first = jnp.concatenate([rows(0, wide), folded(0, SPAN, wide)], axis=0)
+    first = rows(0, 0, wide)
+    zeros = jnp.zeros((first.shape[0], SPAN), first.dtype)
     store(0, jnp.concatenate([zeros, first], axis=1))
     lax.fori_loop(1, columns // wide, piece, 0)
-    last = [rows(columns - SPAN, SPAN), folded(FOLDS - 1, columns // FOLDS, SPAN)]
-    last = jnp.concatenate([jnp.concatenate(last, axis=0), zeros], axis=1)
-    strip[columns // SPAN] = spectra(last[:, SPAN - reach : 2 * SPAN - reach])
+    last = jnp.concatenate([rows(columns // wide, columns - SPAN, SPAN), zeros], axis=1)
+    use(columns // SPAN, last[:, SPAN - reach : 2 * SPAN - reach])
+
+
+def transform_own(reach, rows_in, exposure, sums):
+    def use(entry, window):
+        part = jnp.dot(
+            rows_in[...][:, : exposure.shape[0]], window, preferred_element_type=jnp.float32
+        )
+        for tile in range(window.shape[1] // SPAN):
+            sums[entry + tile] = part[:, tile * SPAN : (tile + 1) * SPAN]
+
+    rows = lambda number, begin, width: exposure[:, pl.ds(begin, width)]
+    each_window(reach, exposure.shape[1], rows, use)
+
+
+def transform_halos(reach, rows_in, exposure, edges, folds, sums, strip):
+    columns = exposure.shape[1]
+    per_fold = columns // FOLDS // (4 * SPAN)
+    fold_of_row = lax.broadcasted_iota(jnp.int32, (EDGE, 1), 0) // (EDGE // FOLDS)
+
+    def rows(number, begin, width):
+        fold = jnp.minimum(number // per_fold, FOLDS - 1)
+        inside = pl.multiple_of(begin + SPAN - fold * (columns // FOLDS), SPAN)
+        mine = fold_of_row == fold
+        halves = [ref[:, pl.ds(begin, width)] for ref in edges]
+        halves += [jnp.where(mine, ref[:, pl.ds(inside, width)], 0) for ref in folds]
+        return jnp.concatenate(halves, axis=0)
+
+    def use(entry, window):
+        part = jnp.dot(
+            rows_in[...][:, exposure.shape[0] :], window, preferred_element_type=jnp.float32
+        )
+        for tile in range(window.shape[1] // SPAN):
+            total = part[:, tile * SPAN : (tile + 1) * SPAN] + sums[entry + tile]
+            strip[entry + tile] = total.astype(strip.dtype)
+
+    each_window(reach, columns, rows, use)
 
 
 def match_group(
-    step, route_smem, rows_out, cols_in, cols_out, row_wave, col_wave, coef_ref,
+    begin, size, route_smem, rows_out, cols_in, cols_out, row_wave, col_wave, coef_ref,
     strip, rows_ref, cols_ref, spectrum, response, warps, waves, warped,
 ):
     low = row_wave.shape[0] // 2
     side = warped.shape[1]
-    numbers = [route_smem[0, step * GROUP + q] for q in range(GROUP)]
+    numbers = [route_smem[0, begin + q] for q in range(size)]
+    depth = size * 2 * low
     windows = [jnp.concatenate([strip[number], strip[number + 1]], axis=1) for number in numbers]
-    spectrum[...] = jnp.dot(
+    spectrum[:depth] = jnp.dot(
         jnp.concatenate(windows, axis=0), cols_in[...], preferred_element_type=jnp.float32
     )
     scaled = [(row_wave[...] * coef_ref[number]).astype(jnp.bfloat16) for number in numbers]
-    response[...] = jnp.dot(
+    response[:depth] = jnp.dot(
         jnp.concatenate(scaled, axis=0), col_wave[...], preferred_element_type=jnp.float32
     )
-    warps[...] = jnp.dot(
+    warps[: size * side] = jnp.dot(
         jnp.concatenate([rows_ref[number] for number in numbers], axis=0),
         rows_out[...],
         preferred_element_type=jnp.float32,
     ).astype(jnp.bfloat16)
-    for q in range(GROUP):
+    for q in range(size):
         top = slice(q * 2 * low, q * 2 * low + low)
         end = slice(q * 2 * low + low, (q + 1) * 2 * low)
         p_re, p_im = spectrum[top, :SPAN], spectrum[top, SPAN:]
@@ -203,11 +215,11 @@
         waves[q * side : (q + 1) * side, :] = jnp.dot(
             warps[q * side : (q + 1) * side, :], stacked, preferred_element_type=jnp.float32
         ).astype(jnp.bfloat16)
-    across = jnp.dot(waves[...], cols_out[...], preferred_element_type=jnp.float32).astype(
+    across = jnp.dot(waves[: size * side], cols_out[...], preferred_element_type=jnp.float32).astype(
         jnp.bfloat16
     )
-    for q in range(GROUP):
-        warped[step * GROUP + q] = lax.dot_general(
+    for q in range(size):
+        warped[begin + q] = lax.dot_general(
             across[q * side : (q + 1) * side],
             cols_ref[numbers[q]],
             (((1,), (1,)), ((), ())),
@@ -247,7 +259,7 @@
 def coadd_kernel(
     reach, capacity, places, exposure_hbm, rows_hbm, cols_hbm, tables_hbm,
     row_bases, col_bases, coefficients, variance, owner, slot_index, coadd,
-    exposure, before, after, fold_before, fold_after, fold_down, fold_up, strip, tables, wave_table, row_wave, col_wave, coef_ref,
+    exposure, before, after, fold_before, fold_after, fold_down, fold_up, sums, strip, tables, wave_table, row_wave, col_wave, coef_ref,
     route_table, fields, labels,
     spectrum, response, warps, waves, warped, rows_ref, cols_ref,
     label_in, table_int, table_float, weight_sum, weight_in, scale, running,
@@ -390,6 +402,7 @@
         precision=lax.Precision.HIGHEST,
         preferred_element_type=jnp.float32,
     ).astype(col_wave.dtype)
+    transform_own(reach, rows_in, exposure, sums)
     for load in loads[2:]:
         load.wait()
     move.wait()
@@ -404,19 +417,20 @@
         for copy in up:
             copy.wait_recv()
 
-    transform_rows(reach, rows_in, exposure, (before, after), (fold_before, fold_after), strip)
-
-    def group(step, carry):
+    transform_halos(reach, rows_in, exposure, (before, after), (fold_before, fold_after), sums, strip)
+
+    def group(size, step, carry):
         match_group(
-            step, route_smem, rows_out, cols_in, cols_out, row_wave, col_wave, coef_ref,
+            step * size, size, route_smem, rows_out, cols_in, cols_out, row_wave, col_wave, coef_ref,
             strip, rows_ref, cols_ref, spectrum, response, warps, waves, warped,
         )
-        for hop in range(ready):
+        for number in range(size // capacity):
             for part in range(parts):
-                send(part, step * ready + hop)
+                send(part, step * (size // capacity) + number)
         return carry
 
-    lax.fori_loop(0, steps, group, 0)
+    lax.fori_loop(0, ready, functools.partial(group, capacity), 0)
+    lax.fori_loop(1, steps, functools.partial(group, GROUP), 0)
     for part in range(parts):
         each_hop(steps * ready, count - 1, lambda hop, part=part: send(part, hop))
         for r in range(capacity):
@@ -563,6 +577,7 @@
             vmem((EDGE, columns), narrow),
             vmem((EDGE, columns), narrow),
             *[vmem((EDGE, columns // FOLDS + SPAN), narrow)] * 4,
+            vmem((columns // SPAN + 1, spectra, SPAN), wide),
             vmem((columns // SPAN + 1, spectra, SPAN), narrow),
             vmem((places[4][0], 2 * SPAN), narrow),
             vmem(tables.shape, wide),

time: 99.2 us -> 97.2 us (0.980)
  Pallas kernels: 96.7 us -> 93.8 us
    pallas_call x1, Pallas kernels: 96.7 us -> 93.8 us  [body(): pl.pallas_call(functools.partial(coadd_kernel, reach, capacity, places),...]
where the time goes in v7:
time: 97.2 us; the launch traced here: 96.1 us
  Pallas kernels  93.8 us (97%)
  local copies, waits for them, and re-layouts  2.26 us (2%)
    pallas_call x1, Pallas kernels, body(): pl.pallas_call(functools.partial(coadd_kernel, reach, capacity, places),...  93.8 us
    unnamed x1, local copies, waits for them, and re-layouts  2.26 us

profile of v7, /device:TPU:3, one launch (start us, length us, event | category | flops | bytes accessed | tf_op | source)
XLA Modules:
  0.0 96.1 jit_solution(5848967392360658902)
XLA Ops:
  0.0 93.8 %shard_map.100 = f32[4,128,512]{2,1,0:T(8,128)} custom-call(bf16[128,8192]{1,0:T(8,128)(2,1)} %bitcast.9, bf16[64,128,128]{2,1,0:T(8,128)(2,1)} %bitcast.10, bf16[64,128,128]{2,1,0:T(8,128)(2,1)} %bitcast.11, f32[1072,256]{1,0:T(8,128)} %constant.2.clone.tables_hbm, bf16[27,41]{1,0:T(8,128)(2,1)} %row_bases.1, bf16[27,41]{1,0:T(8,128)(2,1)} %col_bases.1, ...), custom_call_target="tpu_custom_call" | custom-call | flops 4294967296 | bytes 10485760 | tf_op jit(solution)/shard_map/pallas_call | solution.py:570
  93.8 2.3 %copy.12 = f32[4,128,512]{2,1,0:T(8,128)} copy(f32[4,128,512]{2,1,0:T(8,128)} %shard_map.100) | data formatting | bytes 2097152

commit v8 on v7

--- a/solution.py
+++ b/solution.py
@@ -485,7 +485,7 @@
             return total
 
         lax.fori_loop(
-            0, arrived[part].shape[0], add, jnp.zeros((high, side), jnp.float32), unroll=4
+            0, arrived[part].shape[0], add, jnp.zeros((high, side), jnp.float32), unroll=16
         )
 
         def take(slot, carry):
@@ -495,7 +495,7 @@
             partial[part][row, place] = total.astype(jnp.bfloat16)
             return carry
 
-        lax.fori_loop(0, tiles * across * across, take, 0, unroll=4)
+        lax.fori_loop(0, tiles * across * across, take, 0, unroll=8)
 
     def finish(part):
         for hop in range(1, peers):

time: 97.2 us -> 96.6 us (level)
  no operation moved by 1% of the time
where the time goes in v8:
time: 96.6 us; the launch traced here: 95.8 us
  Pallas kernels  93.6 us (97%)
  local copies, waits for them, and re-layouts  2.26 us (2%)
    pallas_call x1, Pallas kernels, body(): pl.pallas_call(functools.partial(coadd_kernel, reach, capacity, places),...  93.6 us
    unnamed x1, local copies, waits for them, and re-layouts  2.26 us

profile of v8, /device:TPU:3, one launch (start us, length us, event | category | flops | bytes accessed | tf_op | source)
XLA Modules:
  0.0 95.8 jit_solution(13493617625232919644)
XLA Ops:
  0.0 93.6 %shard_map.100 = f32[4,128,512]{2,1,0:T(8,128)} custom-call(bf16[128,8192]{1,0:T(8,128)(2,1)} %bitcast.9, bf16[64,128,128]{2,1,0:T(8,128)(2,1)} %bitcast.10, bf16[64,128,128]{2,1,0:T(8,128)(2,1)} %bitcast.11, f32[1072,256]{1,0:T(8,128)} %constant.2.clone.tables_hbm, bf16[27,41]{1,0:T(8,128)(2,1)} %row_bases.1, bf16[27,41]{1,0:T(8,128)(2,1)} %col_bases.1, ...), custom_call_target="tpu_custom_call" | custom-call | flops 4294967296 | bytes 10485760 | tf_op jit(solution)/shard_map/pallas_call | solution.py:570
  93.6 2.3 %copy.12 = f32[4,128,512]{2,1,0:T(8,128)} copy(f32[4,128,512]{2,1,0:T(8,128)} %shard_map.100) | data formatting | bytes 2097152

commit v9 on v7

--- a/solution.py
+++ b/solution.py
@@ -432,7 +432,9 @@
     lax.fori_loop(0, ready, functools.partial(group, capacity), 0)
     lax.fori_loop(1, steps, functools.partial(group, GROUP), 0)
     for part in range(parts):
-        each_hop(steps * ready, count - 1, lambda hop, part=part: send(part, hop))
+        first, rest = steps * ready, count - 1 - steps * ready
+        turned = lambda hop, part=part: send(part, first + lax.rem(hop + 4 * part, rest))
+        each_hop(0, rest, turned)
         for r in range(capacity):
             arrived[part][me * capacity + r] = piece(count - 1, r, part)
 

time: 97.2 us -> 97.7 us (level)
  Pallas kernels: 93.8 us -> 95.2 us
    pallas_call x1, Pallas kernels: 93.8 us -> 95.2 us  [body(): pl.pallas_call(functools.partial(coadd_kernel, reach, capacity, places),...]
where the time goes in v9:
time: 97.7 us; the launch traced here: 97.5 us
  Pallas kernels  95.2 us (97%)
  local copies, waits for them, and re-layouts  2.26 us (2%)
    pallas_call x1, Pallas kernels, body(): pl.pallas_call(functools.partial(coadd_kernel, reach, capacity, places),...  95.2 us
    unnamed x1, local copies, waits for them, and re-layouts  2.26 us

profile of v9, /device:TPU:3, one launch (start us, length us, event | category | flops | bytes accessed | tf_op | source)
XLA Modules:
  0.0 97.5 jit_solution(8983489712329526554)
XLA Ops:
  0.0 95.2 %shard_map.100 = f32[4,128,512]{2,1,0:T(8,128)} custom-call(bf16[128,8192]{1,0:T(8,128)(2,1)} %bitcast.9, bf16[64,128,128]{2,1,0:T(8,128)(2,1)} %bitcast.10, bf16[64,128,128]{2,1,0:T(8,128)(2,1)} %bitcast.11, f32[1072,256]{1,0:T(8,128)} %constant.2.clone.tables_hbm, bf16[27,41]{1,0:T(8,128)(2,1)} %row_bases.1, bf16[27,41]{1,0:T(8,128)(2,1)} %col_bases.1, ...), custom_call_target="tpu_custom_call" | custom-call | flops 4294967296 | bytes 10485760 | tf_op jit(solution)/shard_map/pallas_call | solution.py:572
  95.2 2.3 %copy.12 = f32[4,128,512]{2,1,0:T(8,128)} copy(f32[4,128,512]{2,1,0:T(8,128)} %shard_map.100) | data formatting | bytes 2097152
